TPU v7x, 128 devices: a whole 4x4x4 slice. The times are simulated.
128 devices in a mesh: seq: 32 (over z, y, core), head: 4 (over x).
Axes of the slice: x: 4, y: 4, z: 4, core: 2. Of those that a mesh axis runs over, the one named last changes fastest.
Arguments:
- hidden_in: bfloat16 [4096, 2048], P('seq'), may hold values from -6 to 6
- cotangent: bfloat16 [4096, 2048], P('seq'), may hold values from -6 to 6
- segment_ids: int32 [4096], replicated, may hold values from 0 to 4, as said below
- norm_gain: float32 [2, 2048], replicated, may hold values from 0.5 to 1.5
- weight_zx: bfloat16 [2, 2048, 2, 4096], P(None, None, None, 'head'), may hold values from -0.125 to 0.125
- weight_bc: bfloat16 [2, 2048, 256], replicated, may hold values from -0.125 to 0.125
- weight_dt: bfloat16 [2, 2048, 64], P(None, None, 'head'), may hold values from -0.125 to 0.125
- dt_bias: float32 [2, 64], P(None, 'head'), may hold values from -3 to -0.5
- a_log: float32 [2, 64], P(None, 'head'), may hold values from -12 to 0
- skip_scale: float32 [2, 64], P(None, 'head'), may hold values from 0.5 to 1.5
- conv_x: float32 [2, 4, 4096], P(None, None, 'head'), may hold values from -3 to 3
- conv_x_bias: float32 [2, 4096], P(None, 'head'), may hold values from -1.8 to 1.8
- conv_bc: float32 [2, 4, 256], replicated, may hold values from -3 to 3
- conv_bc_bias: float32 [2, 256], replicated, may hold values from -1.8 to 1.8
- gate_gain: float32 [2, 4096], P(None, 'head'), may hold values from 0.5 to 1.5
- weight_out: bfloat16 [2, 4096, 2048], P(None, 'head'), may hold values from -0.09375 to 0.09375
Outputs:
- out_hidden: bfloat16 [4096, 2048], P('seq')
- grad_in: bfloat16 [4096, 2048], P('seq')
- grad_norm_gain: float32 [2, 2048], P(None, 'seq')
- grad_weight_zx: float32 [2, 2048, 2, 4096], P(None, 'seq', None, 'head')
- grad_weight_bc: float32 [2, 2048, 256], P(None, 'seq')
- grad_weight_dt: float32 [2, 2048, 64], P(None, 'seq', 'head')
- grad_dt_bias: float32 [2, 64], P(None, 'head')
- grad_a_log: float32 [2, 64], P(None, 'head')
- grad_skip_scale: float32 [2, 64], P(None, 'head')
- grad_conv_x: float32 [2, 4, 4096], P(None, None, 'head')
- grad_conv_x_bias: float32 [2, 4096], P(None, 'head')
- grad_conv_bc: float32 [2, 4, 256], replicated
- grad_conv_bc_bias: float32 [2, 256], replicated
- grad_gate_gain: float32 [2, 4096], P(None, 'head')
- grad_weight_out: float32 [2, 4096, 2048], P(None, 'head', 'seq')
Inputs may be any that keep to these rules, and one draw needn't show every extreme that they name: `segment_ids`: ids never fall along the sequence, start at 0, and end at (4096 - 1) // 1000; every document but the first and the last holds 100 to 1000 tokens.
All inputs are finite; a program needn't handle non-finite values.
Results may differ from a plain program's by a relative error of at most 0.025.
Values may be sent and summed in bfloat16 or wider, within the bound.
A program may use at most 256 MiB of HBM per device.

v0:
```python
import math

import jax
import jax.numpy as jnp
from jax import lax
from jax.sharding import Mesh
from jax.sharding import PartitionSpec as P

D = 2048
HEAD_DIM = 64
STATE = 128
LAYERS = 2
INNER = 4096
SEQ = ("seq_0", "seq_1", "seq_2")


EPSILON = 1e-05


def from_behind(block, axis, distance):
    devices = range(lax.axis_size(axis))
    route = [(i - distance, i) for i in devices if i - distance in devices]
    return lax.ppermute(block, axis, route)


def nothing_yet(array, identity):
    return jax.tree.map(
        lambda a, e: jnp.broadcast_to(jnp.asarray(e, a.dtype), a.shape), array, identity
    )


def carried_in(array, axes, combine, identity):
    before = start = nothing_yet(array, identity)
    subtotal = array
    for axis in reversed(axes):
        devices, position = (lax.axis_size(axis), lax.axis_index(axis))
        pieces = jax.tree.map(lambda part: lax.all_gather(part, axis), subtotal)
        inside, subtotal = (start, start)
        for k in range(devices):
            passed = k < position
            subtotal = combine(subtotal, jax.tree.map(lambda part: part[k], pieces))
            inside = jax.tree.map(lambda new, old: jnp.where(passed, new, old), subtotal, inside)
        before = combine(inside, before)
    return before


def copy_for_each(array, axis):
    devices = lax.axis_size(axis)
    return lax.all_to_all(
        jnp.broadcast_to(array[None], (devices, *array.shape)), axis, 0, 0, tiled=True
    )


def of_everyone(array, axis):
    everything = copy_for_each(array, axis)
    return jnp.sum(everything, axis=0)


def entering_2(array, axes, combine, identity):
    before = start = nothing_yet(array, identity)
    subtotal = array
    for axis in reversed(axes):
        devices, position = (lax.axis_size(axis), lax.axis_index(axis))
        pieces = jax.tree.map(
            lambda part, kind: lax.all_gather(part.astype(kind), axis),
            subtotal,
            jax.tree.map(lambda a: jnp.bfloat16 if a.dtype == jnp.float32 else a.dtype, array),
        )
        inside, subtotal = (start, start)
        for k in reversed(range(devices)):
            passed = k > position
            subtotal = combine(
                subtotal, jax.tree.map(lambda part, own: part[k].astype(own.dtype), pieces, array)
            )
            inside = jax.tree.map(lambda new, old: jnp.where(passed, new, old), subtotal, inside)
        before = combine(inside, before)
    return before


def taken_together(array, axis):
    return copy_for_each(array, axis).astype(jnp.float32).sum(axis=0)


def sent_together(arrays, axis, dim, along):
    widths = [math.prod(a.shape[along:]) for a in arrays]
    both = jnp.concatenate(
        [a.reshape(*a.shape[:along], w) for a, w in zip(arrays, widths)], axis=along
    )
    result = lax.psum_scatter(both, axis, scatter_dimension=dim, tiled=True)
    pieces = jnp.split(result, [sum(widths[:k]) for k in range(1, len(widths))], axis=along)
    return tuple(
        (b.reshape(*result.shape[:along], *a.shape[along:]) for a, b in zip(arrays, pieces))
    )


def rounded(tensor):
    return lax.optimization_barrier(tensor.astype(jnp.bfloat16)).astype(jnp.float32)


def convolve(extended, weights, biases, extended_ids):
    taps = weights.shape[0]
    length = extended.shape[0] - (taps - 1)
    current = extended_ids[taps - 1 :]
    totals = jnp.zeros((length, extended.shape[1]), extended.dtype) + biases[None, :]
    for offset in range(taps):
        keep = (extended_ids[offset : offset + length] == current)[:, None]
        totals = totals + jnp.where(
            keep, weights[offset][None, :] * extended[offset : offset + length], 0.0
        )
    return jax.nn.silu(totals)


def block_step(carried, block_inputs):
    ssm_state, prior_id = carried
    values, keys, queries, steps, rates, block_ids = block_inputs
    cumul = jnp.cumsum(rates, axis=0)
    length = rates.shape[0]
    row_index = lax.broadcasted_iota(jnp.int32, (length, length), 0)
    col_index = lax.broadcasted_iota(jnp.int32, (length, length), 1)
    allowed = ((row_index >= col_index) & (block_ids[:, None] == block_ids[None, :]))[:, :, None]
    spread = cumul[:, None, :] - cumul[None, :, :]
    decays = jnp.where(allowed, jnp.exp(jnp.where(allowed, spread, 0.0)), 0.0)
    intersection = jnp.dot(queries, keys.T)
    mixing = intersection[:, :, None] * decays * steps[None, :, :]
    outputs = jnp.einsum("tsh,shp->thp", mixing, values)
    carry_flag = (block_ids == prior_id).astype(rates.dtype)
    entering = jnp.exp(cumul) * carry_flag[:, None]
    outputs = outputs + jnp.einsum("tn,th,hpn->thp", queries, entering, ssm_state)
    ending = (block_ids == block_ids[-1]).astype(rates.dtype)
    leaving = jnp.exp(cumul[-1][None, :] - cumul) * ending[:, None] * steps
    new_state = entering[-1][:, None, None] * ssm_state + jnp.einsum(
        "sh,shp,sn->hpn", leaving, values, keys
    )
    return ((new_state, block_ids[-1]), outputs)


def make_lead(block_ids, prior_id):

    def lead(values, keys, queries, dt_raw, dt_offset, decay_log):
        steps = jax.nn.softplus(dt_raw + dt_offset[None, :])
        rates = -steps * jnp.exp(decay_log)[None, :]
        tokens = values.shape[0]
        block_len = min(256, tokens)
        blocks_total = tokens // block_len

        def split_blocks(tensor):
            return tensor.reshape((blocks_total, block_len) + tensor.shape[1:])

        initial = jnp.zeros((values.shape[1], values.shape[2], keys.shape[1]), jnp.float32)
        carried, outputs = lax.scan(
            jax.checkpoint(block_step),
            (initial, block_ids[0]),
            tuple(
                (
                    split_blocks(tensor)
                    for tensor in (values, keys, queries, steps, rates, block_ids)
                )
            ),
        )
        carry_flag = (block_ids == prior_id).astype(jnp.float32)
        entry = jnp.exp(jnp.cumsum(rates, axis=0)) * carry_flag[:, None]
        return (outputs.reshape(values.shape), carried[0], entry)

    return lead


def middle(local_out, entry, queries, values, gate_z, state_in, skip_row):
    mixed = (
        local_out
        + jnp.einsum("tn,th,hpn->thp", queries, entry, state_in)
        + skip_row[None, :, None] * values
    )
    return mixed.reshape(mixed.shape[0], -1) * jax.nn.silu(gate_z)


def chain(earlier, later):
    return (earlier[0] * later[0], later[0][:, None, None] * earlier[1] + later[1])


def forward_layer(resid, parameters, extended_ids, block_ids, prior_id):
    (
        norm_row,
        zx_matrix,
        bc_matrix,
        dt_matrix,
        dt_offset,
        decay_log,
        skip_row,
        xconv_taps,
        xconv_bias,
        bconv_taps,
        bconv_bias,
        gate_row,
        out_matrix,
    ) = parameters
    tokens = resid.shape[0]
    taps = xconv_taps.shape[0]
    local_inner = xconv_taps.shape[1]
    inv_root = lax.rsqrt(jnp.mean(resid * resid, axis=1, keepdims=True) + EPSILON)
    normed = (resid * inv_root * norm_row[None, :]).astype(jnp.bfloat16)
    projected = jnp.einsum("td,dki->tki", normed, zx_matrix, preferred_element_type=jnp.float32)
    bc_raw = jnp.dot(normed, bc_matrix, preferred_element_type=jnp.float32)
    dt_raw = jnp.dot(normed, dt_matrix, preferred_element_type=jnp.float32)
    conv_in = jnp.concatenate([projected[:, 1], bc_raw], axis=1)
    edge_rows = from_behind(conv_in[tokens - (taps - 1) :], SEQ, 1)
    extended = jnp.concatenate([edge_rows, conv_in], axis=0)
    conv_taps = jnp.concatenate([xconv_taps, bconv_taps], axis=1)
    conv_bias = jnp.concatenate([xconv_bias, bconv_bias])
    activated, conv_pull = jax.vjp(
        lambda rows_in, tap_rows, bias_row: convolve(rows_in, tap_rows, bias_row, extended_ids),
        extended,
        conv_taps,
        conv_bias,
    )
    values = rounded(activated[:, :local_inner]).reshape(tokens, local_inner // HEAD_DIM, HEAD_DIM)
    keys = rounded(activated[:, local_inner : local_inner + STATE])
    queries = rounded(activated[:, local_inner + STATE :])
    (local_out, state_end, entry), lead_pull = jax.vjp(
        make_lead(block_ids, prior_id), values, keys, queries, dt_raw, dt_offset, decay_log
    )
    decay_total = entry[-1]
    identity = (jnp.ones_like(decay_total), jnp.zeros_like(state_end))
    prefix = carried_in((decay_total, state_end), SEQ, chain, identity)
    state_in = prefix[1]
    gated, middle_pull = jax.vjp(
        middle, local_out, entry, queries, values, projected[:, 0], state_in, skip_row
    )
    square_sum = of_everyone(jnp.sum(gated * gated, axis=1), "head")
    gate_root = lax.rsqrt(square_sum / INNER + EPSILON)[:, None]
    scaled = (gated * gate_root * gate_row[None, :]).astype(jnp.bfloat16)
    branch = of_everyone(jnp.dot(scaled, out_matrix, preferred_element_type=jnp.float32), "head")
    kept = {
        "resid": resid,
        "inv_root": inv_root,
        "normed": normed,
        "conv_pull": conv_pull,
        "lead_pull": lead_pull,
        "middle_pull": middle_pull,
        "decay_total": decay_total,
        "state_in": state_in,
        "gated": gated,
        "gate_root": gate_root,
        "scaled": scaled,
    }
    return (resid + branch, kept)


def backward_layer(grad_resid, kept, parameters):
    (
        norm_row,
        zx_matrix,
        bc_matrix,
        dt_matrix,
        dt_offset,
        decay_log,
        skip_row,
        xconv_taps,
        xconv_bias,
        bconv_taps,
        bconv_bias,
        gate_row,
        out_matrix,
    ) = parameters
    tokens = grad_resid.shape[0]
    taps = xconv_taps.shape[0]
    local_inner = xconv_taps.shape[1]
    resid = kept["resid"]
    inv_root = kept["inv_root"]
    normed = kept["normed"]
    gated = kept["gated"]
    gate_root = kept["gate_root"]
    grad_branch = grad_resid.astype(jnp.bfloat16)
    grad_out_matrix = jnp.einsum(
        "ti,td->id", kept["scaled"], grad_branch, preferred_element_type=jnp.float32
    )
    grad_scaled = jnp.einsum(
        "td,id->ti", grad_branch, out_matrix, preferred_element_type=jnp.float32
    )
    weighted = grad_scaled * gate_row[None, :]
    grad_gate_row = jnp.sum(grad_scaled * gated * gate_root, axis=0)
    root_sum = of_everyone(jnp.sum(weighted * gated, axis=1), "head")[:, None]
    grad_gated = weighted * gate_root - root_sum * gate_root * gate_root * gate_root * gated / INNER
    (
        grad_local_out,
        grad_entry,
        grad_queries_mid,
        grad_values_mid,
        grad_gate_z,
        grad_state_direct,
        grad_skip,
    ) = kept["middle_pull"](grad_gated)
    decay_total = kept["decay_total"]
    identity = (jnp.ones_like(decay_total), jnp.zeros_like(grad_state_direct))
    suffix = entering_2((decay_total, grad_state_direct), SEQ, chain, identity)
    grad_state_end = suffix[1]
    grad_decay = jnp.sum(grad_state_end * kept["state_in"], axis=(1, 2))
    grad_entry = grad_entry.at[-1].add(grad_decay)
    grad_values_lead, grad_keys, grad_queries_lead, grad_dt_raw, grad_dt_offset, grad_decay_log = (
        kept["lead_pull"]((grad_local_out, grad_state_end, grad_entry))
    )
    grad_activated = jnp.concatenate(
        [
            (grad_values_mid + grad_values_lead).reshape(tokens, local_inner),
            grad_keys,
            grad_queries_mid + grad_queries_lead,
        ],
        axis=1,
    )
    grad_extended, grad_conv_taps, grad_conv_bias = kept["conv_pull"](grad_activated)
    from_right = from_behind(grad_extended[: taps - 1], SEQ, -1)
    grad_conv_in = grad_extended[taps - 1 :] + jnp.concatenate(
        [jnp.zeros((tokens - (taps - 1), grad_extended.shape[1]), jnp.float32), from_right], axis=0
    )
    grad_zx = jnp.stack([grad_gate_z, grad_conv_in[:, :local_inner]], axis=1).astype(jnp.bfloat16)
    grad_dt_round = grad_dt_raw.astype(jnp.bfloat16)
    partial_normed = jnp.einsum(
        "tki,dki->td", grad_zx, zx_matrix, preferred_element_type=jnp.float32
    ) + jnp.einsum("th,dh->td", grad_dt_round, dt_matrix, preferred_element_type=jnp.float32)
    summed_normed, grad_bc_sum, grad_bconv_taps, grad_bconv_bias = (
        taken_together(partial_normed.astype(jnp.bfloat16), "head").astype(jnp.float32),
        taken_together(grad_conv_in[:, local_inner:].astype(jnp.bfloat16), "head").astype(
            jnp.float32
        ),
        taken_together(grad_conv_taps[:, local_inner:].astype(jnp.bfloat16), "head").astype(
            jnp.float32
        ),
        taken_together(grad_conv_bias[local_inner:].astype(jnp.bfloat16), "head").astype(
            jnp.float32
        ),
    )
    grad_bc_round = grad_bc_sum.astype(jnp.bfloat16)
    grad_normed = summed_normed + jnp.einsum(
        "tc,dc->td", grad_bc_round, bc_matrix, preferred_element_type=jnp.float32
    )
    grad_bc_matrix = jnp.einsum(
        "td,tc->dc", normed, grad_bc_round, preferred_element_type=jnp.float32
    )
    gain_weighted = grad_normed * norm_row[None, :]
    grad_norm_row = jnp.sum(grad_normed * resid * inv_root, axis=0)
    grad_below = (
        grad_resid
        + gain_weighted * inv_root
        - resid
        * inv_root
        * inv_root
        * inv_root
        * jnp.sum(gain_weighted * resid, axis=1, keepdims=True)
        / D
    )
    grad_columns = jnp.concatenate(
        [grad_zx.reshape(tokens, 2 * local_inner), grad_dt_round], axis=1
    )
    seq_devices = lax.axis_size(SEQ)
    row_share = D // seq_devices
    feature_slab = lax.all_to_all(normed, SEQ, split_axis=1, concat_axis=0, tiled=True)
    proj_grads = jnp.einsum(
        "tr,tc->rc",
        feature_slab,
        lax.all_gather(grad_columns, SEQ, axis=0, tiled=True),
        preferred_element_type=jnp.float32,
    )
    grad_zx_rows = proj_grads[:, : 2 * local_inner].reshape(row_share, 2, local_inner)
    grad_dt_rows = proj_grads[:, 2 * local_inner :]
    grad_bc_rows, grad_norm_rows, grad_out_cols = (
        *tuple(
            (
                part.astype(jnp.float32)
                for part in sent_together(
                    (grad_bc_matrix.astype(jnp.bfloat16), grad_norm_row.astype(jnp.bfloat16)),
                    SEQ,
                    0,
                    1,
                )
            )
        ),
        lax.psum_scatter(
            grad_out_matrix.astype(jnp.bfloat16), SEQ, scatter_dimension=1, tiled=True
        ).astype(jnp.float32),
    )
    small_sums = (
        of_everyone(grad_dt_offset, SEQ),
        of_everyone(grad_decay_log, SEQ),
        of_everyone(grad_skip, SEQ),
        of_everyone(grad_conv_taps[:, :local_inner], SEQ),
        of_everyone(grad_conv_bias[:local_inner], SEQ),
        of_everyone(grad_gate_row, SEQ),
        of_everyone(grad_bconv_taps, SEQ),
        of_everyone(grad_bconv_bias, SEQ),
    )
    results = (
        grad_norm_rows,
        grad_zx_rows,
        grad_bc_rows,
        grad_dt_rows,
        small_sums[0],
        small_sums[1],
        small_sums[2],
        small_sums[3],
        small_sums[4],
        small_sums[6],
        small_sums[7],
        small_sums[5],
        grad_out_cols,
    )
    return (grad_below, results)


def local(
    hidden_in,
    cotangent,
    segment_ids,
    norm_gain,
    weight_zx,
    weight_bc,
    weight_dt,
    dt_bias,
    a_log,
    skip_scale,
    conv_x,
    conv_x_bias,
    conv_bc,
    conv_bc_bias,
    gate_gain,
    weight_out,
):
    tokens = hidden_in.shape[0]
    taps = conv_x.shape[1]
    padded_ids = jnp.concatenate([jnp.full((taps - 1,), -1, jnp.int32), segment_ids])
    extended_ids = lax.dynamic_slice_in_dim(
        padded_ids, lax.axis_index(SEQ) * tokens, tokens + taps - 1
    )
    block_ids = extended_ids[taps - 1 :]
    prior_id = extended_ids[taps - 2]
    stacked = (
        norm_gain,
        weight_zx,
        weight_bc,
        weight_dt,
        dt_bias,
        a_log,
        skip_scale,
        conv_x,
        conv_x_bias,
        conv_bc,
        conv_bc_bias,
        gate_gain,
        weight_out,
    )
    resid = hidden_in.astype(jnp.float32)
    saved = []
    for layer_index in range(LAYERS):
        parameters = tuple((tensor[layer_index] for tensor in stacked))
        resid, kept = forward_layer(resid, parameters, extended_ids, block_ids, prior_id)
        saved.append(kept)
    grad_resid = cotangent.astype(jnp.float32)
    collected = [None] * LAYERS
    for layer_index in reversed(range(LAYERS)):
        parameters = tuple((tensor[layer_index] for tensor in stacked))
        grad_resid, results = backward_layer(grad_resid, saved[layer_index], parameters)
        collected[layer_index] = results
    merged = [
        jnp.stack([collected[layer_index][position] for layer_index in range(LAYERS)])
        for position in range(13)
    ]
    return (
        resid.astype(jnp.bfloat16),
        grad_resid.astype(jnp.bfloat16),
        merged[0],
        merged[1],
        merged[2],
        merged[3],
        merged[4],
        merged[5],
        merged[6],
        merged[7],
        merged[8],
        merged[9],
        merged[10],
        merged[11],
        merged[12],
    )


def solution(mesh):
    finer = Mesh(
        mesh.devices.reshape(4, 4, 2, mesh.shape["head"]), ("seq_0", "seq_1", "seq_2", "head")
    )
    in_specs = (
        P(SEQ, None),
        P(SEQ, None),
        P(),
        P(),
        P(None, None, None, "head"),
        P(),
        P(None, None, "head"),
        P(None, "head"),
        P(None, "head"),
        P(None, "head"),
        P(None, None, "head"),
        P(None, "head"),
        P(),
        P(),
        P(None, "head"),
        P(None, "head", None),
    )
    out_specs = (
        P(SEQ, None),
        P(SEQ, None),
        P(None, SEQ),
        P(None, SEQ, None, "head"),
        P(None, SEQ, None),
        P(None, SEQ, "head"),
        P(None, "head"),
        P(None, "head"),
        P(None, "head"),
        P(None, None, "head"),
        P(None, "head"),
        P(),
        P(),
        P(None, "head"),
        P(None, "head", SEQ),
    )
    return jax.shard_map(local, mesh=finer, in_specs=in_specs, out_specs=out_specs, check_vma=False)
```

profile of v0, /device:TPU:1, one launch (start us, length us, event | category | flops | bytes accessed | tf_op | source)
XLA Modules:
  0.0 1102.7 jit_solution(2315803743143499691)
XLA Ops:
  7.2 14.0 %fusion.357 = (bf16[1,2048,2,1024]{3,2,1,0:T(2,128)(2,1)}, bf16[1,2048,2,1024]{3,2,1,0:T(2,128)(2,1)S(1)}) fusion(bf16[2,2048,2,1024]{3,2,1,0:T(2,128)(2,1)} %param.25), kind=kLoop, calls=%fused_computation.746 | loop fusion | bytes 33554432 | tf_op jit(solution)/shard_map/slice | solution.py:452
  43.6 7.9 all-gather.5
  58.5 31.3 %all-gather.29.cloned.1.call-done = f32[4,16,64,128]{3,2,1,0:T(8,128)} async-done(((f32[1,16,64,128]{3,2,1,0:T(8,128)}), f32[4,16,64,128]{3,2,1,0:T(8,128)}) %all-gather.29.cloned.1.call-update) | async-done | bytes 2097168 | tf_op jit(solution)/shard_map/all_gather | solution.py:37
  95.3 8.1 all-gather.6
  109.2 14.5 %all-gather.31.cloned.1.call-done = f32[4,16,64,128]{3,2,1,0:T(8,128)} async-done(((f32[1,16,64,128]{3,2,1,0:T(8,128)}), f32[4,16,64,128]{3,2,1,0:T(8,128)}) %all-gather.31.cloned.1.call-update) | async-done | bytes 2097168 | tf_op jit(solution)/shard_map/all_gather | solution.py:37
  148.8 46.1 %all-to-all-done.1 = f32[4,128,2048]{2,1,0:T(8,128)} async-done(((f32[4,128,2048]{2,1,0:T(8,128)}), f32[4,128,2048]{2,1,0:T(8,128)}, u32[]{:S(2)}, u32[]{:S(2)}) %all-to-all-start.1) | async-done | bytes 4194336 | tf_op jit(solution)/shard_map/all_to_all | solution.py:49
  224.6 8.3 all-gather.8
  235.8 30.9 %all-gather.33.cloned.1.call-done = f32[4,16,64,128]{3,2,1,0:T(8,128)} async-done(((f32[1,16,64,128]{3,2,1,0:T(8,128)}), f32[4,16,64,128]{3,2,1,0:T(8,128)}) %all-gather.33.cloned.1.call-update) | async-done | bytes 2097168 | tf_op jit(solution)/shard_map/all_gather | solution.py:37
  280.0 8.6 all-gather.9
  291.9 8.5 all-gather.35.cloned.1.call-done
  472.1 8.4 all-gather.14
  487.3 8.2 all-to-all-done.5
  523.8 20.8 %all-gather.41.cloned.1.call-done = bf16[4,16,64,128]{3,2,1,0:T(8,128)(2,1)} async-done(((bf16[1,16,64,128]{3,2,1,0:T(8,128)(2,1)}), bf16[4,16,64,128]{3,2,1,0:T(8,128)(2,1)}) %all-gather.41.cloned.1.call-update) | async-done | bytes 1048592 | tf_op jit(solution)/shard_map/all_gather | solution.py:65
  557.1 8.3 all-gather.15
  638.3 23.8 %all-to-all-done.8 = bf16[4,128,2048]{2,1,0:T(8,128)(2,1)S(1)} async-done(((bf16[4,128,2048]{2,1,0:T(8,128)(2,1)}), bf16[4,128,2048]{2,1,0:T(8,128)(2,1)S(1)}, u32[]{:S(2)}, u32[]{:S(2)}) %all-to-all-start.8) | async-done | bytes 2097184 | tf_op jit(solution)/shard_map/all_to_all | solution.py:49
  671.5 11.7 %all_to_all.206 = f32[32,1,16]{2,1,0:T(1,128)S(1)} all-to-all(f32[32,1,16]{2,1,0:T(1,128)S(1)} %broadcast_in_dim.534), channel_id=1, replica_groups=mesh['seq_0'=4,'seq_1'=4,'seq_2'=2,'head'=4] {'seq_0','seq_1','seq_2'}, dimensions={0} | all-to-all | bytes 4096 | tf_op jit(solution)/shard_map/all_to_all | solution.py:49
  683.3 11.3 %all_to_all.207 = f32[32,1,1024]{2,1,0:T(1,128)S(1)} all-to-all(f32[32,1,1024]{2,1,0:T(1,128)S(1)} %broadcast_in_dim.548), channel_id=1, replica_groups=mesh['seq_0'=4,'seq_1'=4,'seq_2'=2,'head'=4] {'seq_0','seq_1','seq_2'}, dimensions={0} | all-to-all | bytes 262144 | tf_op jit(solution)/shard_map/all_to_all | solution.py:49
  706.1 10.9 all_to_all.208
  840.3 7.7 all-to-all-done.20
  865.1 7.7 all-to-all-done.23
  929.2 69.0 %all-gather.47.cloned.1.call-done = bf16[4096,2064]{0,1:T(8,128)(2,1)} async-done(((bf16[128,2064]{0,1:T(8,128)(2,1)}), bf16[4096,2064]{0,1:T(8,128)(2,1)}) %all-gather.47.cloned.1.call-update) | async-done | bytes 16908304 | tf_op jit(solution)/shard_map/all_gather | solution.py:359
  998.2 11.2 %fusion.138 = f32[64,2064]{1,0:T(8,128)S(1)} fusion(bf16[4096,2064]{0,1:T(8,128)(2,1)} %all-gather.47.cloned.1.call-done, bf16[128,32,64]{0,2,1:T(8,128)(2,1)S(1)} %all-to-all-done.11), kind=kOutput, calls=%fused_computation.264 | convolution fusion | flops 1082130432 | bytes 17960960 | tf_op jit(solution)/shard_map/tr,tc->rc/dot_general | solution.py:356
  1010.0 71.9 %all-gather.45.cloned.1.call-done = bf16[4096,2064]{0,1:T(8,128)(2,1)} async-done(((bf16[128,2064]{0,1:T(8,128)(2,1)}), bf16[4096,2064]{0,1:T(8,128)(2,1)}) %all-gather.45.cloned.1.call-update) | async-done | bytes 16908304 | tf_op jit(solution)/shard_map/all_gather | solution.py:359
  1081.9 11.2 %fusion.141 = f32[64,2064]{1,0:T(8,128)S(1)} fusion(bf16[4096,2064]{0,1:T(8,128)(2,1)} %all-gather.45.cloned.1.call-done, bf16[128,32,64]{0,2,1:T(8,128)(2,1)S(1)} %all-to-all-done.10), kind=kOutput, calls=%fused_computation.267 | convolution fusion | flops 1082130432 | bytes 17960960 | tf_op jit(solution)/shard_map/tr,tc->rc/dot_general | solution.py:356
  (964 shorter events, 624.3 us)
Async XLA Ops:
  7.2 48.5 %all-gather.49.cloned.1.call-start = ((), (), s32[]{:S(2)}) async-start(), calls=%async_computation.48 | async-start | bytes 1572864 | tf_op jit(solution)/shard_map/all_gather | solution.py:37
  41.8 48.0 %all-gather.29.cloned.1.call-start = ((), (), s32[]{:S(2)}) async-start(), calls=%async_computation.36 | async-start | bytes 2621440 | tf_op jit(solution)/shard_map/all_gather | solution.py:37
  57.9 65.8 %all-gather.31.cloned.1.call-start = ((), (), s32[]{:S(2)}) async-start(), calls=%async_computation.37 | async-start | bytes 2621440 | tf_op jit(solution)/shard_map/all_gather | solution.py:37
  143.2 51.8 %all-to-all-start.1 = ((f32[4,128,2048]{2,1,0:T(8,128)}), f32[4,128,2048]{2,1,0:T(8,128)}, u32[]{:S(2)}, u32[]{:S(2)}) async-start(f32[4,128,2048]{2,1,0:T(8,128)} %broadcast_in_dim.516), calls=%async_computation.1 | async-start | bytes 8388608 | tf_op jit(solution)/shard_map/all_to_all | solution.py:49
  148.2 85.4 %all-gather.51.cloned.1.call-start = ((), (), s32[]{:S(2)}) async-start(), calls=%async_computation.49 | async-start | bytes 1572864 | tf_op jit(solution)/shard_map/all_gather | solution.py:37
  222.0 44.6 %all-gather.33.cloned.1.call-start = ((), (), s32[]{:S(2)}) async-start(), calls=%async_computation.38 | async-start | bytes 2621440 | tf_op jit(solution)/shard_map/all_gather | solution.py:37
  235.7 64.8 %all-gather.35.cloned.1.call-start = ((), (), s32[]{:S(2)}) async-start(), calls=%async_computation.39 | async-start | bytes 2621440 | tf_op jit(solution)/shard_map/all_gather | solution.py:37
  326.3 39.6 %all-gather.37.cloned.1.call-start = ((), (), s32[]{:S(2)}) async-start(), calls=%async_computation.40 | async-start | bytes 1310720 | tf_op jit(solution)/shard_map/all_gather | solution.py:65
  344.7 48.1 %all-gather.39.cloned.1.call-start = ((), (), s32[]{:S(2)}) async-start(), calls=%async_computation.41 | async-start | bytes 1310720 | tf_op jit(solution)/shard_map/all_gather | solution.py:65
  377.3 74.0 %all-to-all-start.3 = ((f32[4,128,2048]{2,1,0:T(8,128)}), f32[4,128,2048]{2,1,0:T(8,128)}, u32[]{:S(2)}, u32[]{:S(2)}) async-start(f32[4,128,2048]{2,1,0:T(8,128)} %broadcast_in_dim.518), calls=%async_computation.3 | async-start | bytes 8388608 | tf_op jit(solution)/shard_map/all_to_all | solution.py:49
  464.9 30.6 %all-to-all-start.5 = ((bf16[4,128,2048]{2,1,0:T(8,128)(2,1)}), bf16[4,128,2048]{2,1,0:T(8,128)(2,1)}, u32[]{:S(2)}, u32[]{:S(2)}) async-start(bf16[4,128,2048]{2,1,0:T(8,128)(2,1)} %broadcast_in_dim.522), calls=%async_computation.5 | async-start | bytes 4194304 | tf_op jit(solution)/shard_map/all_to_all | solution.py:49
  510.4 34.3 %all-gather.41.cloned.1.call-start = ((), (), s32[]{:S(2)}) async-start(), calls=%async_computation.42 | async-start | bytes 1310720 | tf_op jit(solution)/shard_map/all_gather | solution.py:65
  523.7 56.2 %all-gather.43.cloned.1.call-start = ((), (), s32[]{:S(2)}) async-start(), calls=%async_computation.43 | async-start | bytes 1310720 | tf_op jit(solution)/shard_map/all_gather | solution.py:65
  547.0 336.5 %reduce-scatter.15.cloned.1.call-start = ((), (), s32[]{:S(2)}) async-start(), calls=%async_computation.51 | async-start | bytes 1622016
  552.4 364.0 %reduce-scatter.11.cloned.1.call-start = ((), (), s32[]{:S(2)}) async-start(), calls=%async_computation.47 | async-start | bytes 4325376 | tf_op jit(solution)/shard_map/reduce_scatter | solution.py:376
  557.1 359.4 %reduce-scatter.9.cloned.1.call-start = ((), (), s32[]{:S(2)}) async-start(), calls=%async_computation.46 | async-start | bytes 4325376 | tf_op jit(solution)/shard_map/reduce_scatter | solution.py:376
  631.6 30.6 %all-to-all-start.8 = ((bf16[4,128,2048]{2,1,0:T(8,128)(2,1)}), bf16[4,128,2048]{2,1,0:T(8,128)(2,1)S(1)}, u32[]{:S(2)}, u32[]{:S(2)}) async-start(bf16[4,128,2048]{2,1,0:T(8,128)(2,1)} %broadcast_in_dim.527), calls=%async_computation.8 | async-start | bytes 4194304 | tf_op jit(solution)/shard_map/all_to_all | solution.py:49
  635.9 282.3 %reduce-scatter.13.cloned.1.call-start = ((), (), s32[]{:S(2)}) async-start(), calls=%async_computation.50 | async-start | bytes 1622016
  667.7 330.5 %all-gather.47.cloned.1.call-start = ((), (), s32[]{:S(2)}) async-start(), calls=%async_computation.45 | async-start | bytes 17436672 | tf_op jit(solution)/shard_map/all_gather | solution.py:359
  669.0 412.9 %all-gather.45.cloned.1.call-start = ((), (), s32[]{:S(2)}) async-start(), calls=%async_computation.44 | async-start | bytes 17436672 | tf_op jit(solution)/shard_map/all_gather | solution.py:359
  873.7 17.0 %all-to-all-start.19 = ((f32[32,4,1024]{2,1,0:T(4,128)}), f32[32,4,1024]{2,1,0:T(4,128)}, u32[]{:S(2)}, u32[]{:S(2)}) async-start(f32[32,4,1024]{2,1,0:T(4,128)} %broadcast_in_dim.536), calls=%async_computation.19 | async-start | bytes 1048576 | tf_op jit(solution)/shard_map/all_to_all | solution.py:49
  891.6 16.3 %all-to-all-start.18 = ((f32[32,4,1024]{2,1,0:T(4,128)}), f32[32,4,1024]{2,1,0:T(4,128)S(1)}, u32[]{:S(2)}, u32[]{:S(2)}) async-start(f32[32,4,1024]{2,1,0:T(4,128)} %broadcast_in_dim.535), calls=%async_computation.18 | async-start | bytes 1048576 | tf_op jit(solution)/shard_map/all_to_all | solution.py:49
  908.7 15.7 %all-to-all-start.11 = ((bf16[128,32,64]{0,2,1:T(8,128)(2,1)}), bf16[128,32,64]{0,2,1:T(8,128)(2,1)S(1)}, u32[]{:S(2)}, u32[]{:S(2)}) async-start(bf16[128,32,64]{0,2,1:T(8,128)(2,1)} %bitcast.990), calls=%async_computation.11 | async-start | bytes 1048576 | tf_op jit(solution)/shard_map/all_to_all | solution.py:355
  924.4 85.5 %all-to-all-start.10 = ((bf16[128,32,64]{0,2,1:T(8,128)(2,1)}), bf16[128,32,64]{0,2,1:T(8,128)(2,1)S(1)}, u32[]{:S(2)}, u32[]{:S(2)}) async-start(bf16[128,32,64]{0,2,1:T(8,128)(2,1)} %bitcast.989), calls=%async_computation.10 | async-start | bytes 1048576 | tf_op jit(solution)/shard_map/all_to_all | solution.py:355
  (265 other events, 4738.7 us)
Sparse Core Ops, SparseCore 0:
  41.9 13.7 all-gather.48
  58.0 31.7 all-gather.28
  92.6 31.0 all-gather.30
  222.1 10.3 all-gather.50
  235.8 30.8 all-gather.32
  269.3 31.0 all-gather.34
  344.9 20.9 all-gather.36
  368.3 24.4 all-gather.38
  523.9 20.7 all-gather.40
  547.1 24.4 all-gather.42
  575.1 78.2 reduce-scatter.14
  656.9 81.0 reduce-scatter.10
  742.1 81.5 reduce-scatter.8
  827.0 81.0 reduce-scatter.12
  910.1 88.0 all-gather.46
  1000.2 81.5 all-gather.44
where the time goes:
time: 1120 us; the launch traced here: 1100 us
  waiting for transfers between devices  453 us (40%)
  other arithmetic  142 us (13%)
  starting transfers between devices  139 us (12%)
  matrix products  122 us (11%)
  blocking collectives  120 us (11%)
  local copies, waits for them, and re-layouts  109 us (10%)
  between operations  18 us (2%)
    all_to_all x26, waiting for transfers between devices, copy_for_each(): lax.all_to_all(jnp.broadcast_to(array[None], (devices, *array.shape)), ax...  188 us
    all_gather x2, waiting for transfers between devices, backward_layer(): lax.all_gather(grad_columns, SEQ, axis=0, tiled=True)  141 us
    all_to_all x26, starting transfers between devices, copy_for_each(): lax.all_to_all(jnp.broadcast_to(array[None], (devices, *array.shape)), ax...  109 us
    all_gather x6, waiting for transfers between devices, carried_in(): pieces = jax.tree.map(lambda part: lax.all_gather(part, axis), subtotal)  88.8 us
    all_gather x8, blocking collectives, entering_2(): lax.all_gather(part.astype(kind), axis)  43.2 us
    all_to_all x4, blocking collectives, copy_for_each(): lax.all_to_all(jnp.broadcast_to(array[None], (devices, *array.shape)), ax...  40.4 us
    all_gather x6, blocking collectives, carried_in(): pieces = jax.tree.map(lambda part: lax.all_gather(part, axis), subtotal)  36.5 us
    all_gather x4, waiting for transfers between devices, entering_2(): lax.all_gather(part.astype(kind), axis)  31.5 us
  transfers between devices with their start and end apart: 48, of which 36 were waited for; matrix products, arithmetic and copies ran while one was open for 22% of the time, Pallas kernels for 0%

commit v1 on v0

v1 whole, which is shorter than its diff:
```python
import types

import jax
import jax.numpy as jnp
from jax import lax
from jax.experimental import pallas as pl
from jax.experimental.pallas import tpu as pltpu
from jax.sharding import Mesh
from jax.sharding import PartitionSpec as P

D = 2048
INNER = 4096
IL = 1024
TOK = 128
ST = 128
HL = 16
NS = 32
NX = 4
HALO = 16
SEQ = ("z", "y", "c")
EPS = 1e-05
F32 = jnp.float32
BF = jnp.bfloat16
MESH = pl.DeviceIdType.MESH
WIDE, NARROW = 1024, 768


def dot(a, b, ca, cb):
    return lax.dot_general(a, b, (((ca,), (cb,)), ((), ())), preferred_element_type=F32)


def nn(a, b):
    return dot(a, b, 1, 0)


def nt(a, b):
    return dot(a, b, 1, 1)


def tn(a, b):
    return dot(a, b, 0, 0)


def pieces(a, count):
    out = []
    for _ in range(count):
        p = a.astype(BF)
        out.append(p)
        a = a - p.astype(F32)
    return out


def split_left(f, a, exact, count=2):
    return sum(f(p, exact) for p in pieces(a, count))


def split_right(f, exact, a, count=2):
    return sum(f(exact, p) for p in pieces(a, count))


def sigmoid(v):
    return 1.0 / (1.0 + jnp.exp(-v))


def seq_at(s):
    return {"z": s // 8, "y": lax.rem(s // 2, 4), "c": lax.rem(s, 2)}


def position():
    return lax.axis_index("z") * 8 + lax.axis_index("y") * 2 + lax.axis_index("c")


def lanes(j, width=128, base=0):
    return pl.ds(pl.multiple_of(base + j * width, 128), width)


def wait_for(ref, sem):
    pltpu.make_async_copy(ref, ref, sem).wait()


IN = dict(
    hid=0, cot=0, idc=0, idr=0, ng=0, gg=0, hp=0, ct=0, wzx_h=1, wbc_h=1, wdt_h=1, wout_h=1
)
OUT = dict(
    oh=((TOK, D), BF, 1),
    gi=((TOK, D), BF, 1),
    zx_o=((2, 2, 64, IL), F32, 1),
    out_o=((2, 64, IL), F32, 1),
    bc_o=((2, 64, 256), F32, 1),
    dt_o=((2, 64, 128), F32, 1),
    sums=((NS, 8, 128), F32, 0),
)
SCRATCH = dict(
    wz=((2, 2, 4, 4, 128, IL), BF),
    wb=((2, D, 256), BF),
    wd=((2, HL, D), BF),
    wo=((2, 8, 128, D), BF),
    nrm=((2, HALO + TOK, D), BF),
    dbr0=((TOK, D), BF),
    z=((2, TOK, IL), F32),
    v=((2, HALO + TOK, 1280), F32),
    xbc=((2, TOK, 1280), BF),
    xdt=((2, TOK, IL), BF),
    L=((2, HL, TOK, TOK), BF),
    G=((2, TOK, TOK), F32),
    y=((2, TOK, IL), F32),
    S=((2, IL, ST), BF),
    dtr=((2, TOK, 128), F32),
    dt=((2, TOK, 128), F32),
    rate=((2, TOK, 128), F32),
    cum=((2, TOK, 128), F32),
    entry=((2, TOK, 128), F32),
    wl=((2, TOK, 128), F32),
    dtot=((2, 128, 128), F32),
    q=((2, TOK, 128), F32),
    skE=((2, 8, IL), F32),
    u=((2, 32, D), F32),
    br=((32, D), F32),
    mk=((3, TOK, 128), F32),
    mkb=((3, TOK, 128), F32),
    E=((128, IL), BF),
    Et=((IL, 128), BF),
    tri=((TOK, TOK), BF),
    sb=((NS, 48, 128), BF),
    rb=((2, NS, 48, 128), BF),
    eb=((NS, 32, 128), BF),
    sin=((2, NS, 32, 128), BF),
    sbb=((NS, 32, 128), BF),
    rbb=((2, NS, 32, 128), BF),
    lam=((2, NS, 32, 128), BF),
    sq=((2, 8, 128), F32),
    sqx=((2, NX, 8, 128), F32),
    pb=((TOK, D), BF),
    rs=((2, NX, 32, D), BF),
    gs=((TOK, IL), BF),
    ds=((TOK, IL), F32),
    dbc=((TOK, 256), F32),
    dyb=((TOK, IL), BF),
    dye=((TOK, IL), BF),
    U=((TOK, IL), F32),
    rows=((TOK, 128), F32),
    dsk=((8, IL), F32),
    entE=((TOK, IL), F32),
    wlE=((TOK, IL), F32),
    dtE=((TOK, IL), F32),
    dpre=((2, TOK + 8, 1280), F32),
    scol=((TOK, 128), F32),
    du=((32, D), F32),
    edge=((2, 32, D), BF),
    dbp=((TOK, 256), BF),
    bx=((2, NX, TOK, 256), BF),
    ro=((2, TOK, WIDE), BF),
    re=((2, TOK, NARROW), BF),
    nsib=((TOK, D), BF),
    dsib=((TOK, D), BF),
    rsib=((2, TOK, WIDE), BF),
    part=((4, 4, 128, WIDE), BF),
    land=((4, 2, 4, 128, 512), BF),
    total=((128, WIDE), F32),
    sm=((NS, 8, 128), F32),
    smr=((NS, 8, 128), F32),
    smt=((8, 128), F32),
    smx=((NX, 8, 128), F32),
)


class K:
    (
        WZ, WX, WB, WD, WO, ST, EN, SB, EB, SQ, RS, RB, AG, HA, DP, SC, OH, GI, NSIB, DSIB, BX,
        SM, SX, SG, OWN,
    ) = range(25)


class J:
    RX, Y1, Z1, Y2, Z2, OUT, OWN = range(7)


def chain_kernel(*refs):
    R = types.SimpleNamespace(**dict(zip([*IN, *OUT, *SCRATCH, "sem", "jsem"], refs)))
    iz, iy, ic, mx = (lax.axis_index(a) for a in ("z", "y", "c", "x"))
    me = position()
    mine = pl.ds(pl.multiple_of(mx * 32, 32), 32)

    def sem(kind, l, side):
        return R.sem.at[kind, l, side]

    def send(src, dst, s, r, to):
        pltpu.make_async_remote_copy(
            src, dst, s, r, device_id=to, device_id_type=MESH
        ).start()

    def exchange(src, dst, kind, l):
        dst[pl.ds(me, 1)] = src[pl.ds(me, 1)]

        @pl.loop(1, NS)
        def _(k):
            d = lax.rem(me + k, NS)
            send(src.at[d], dst.at[me], sem(kind, l, 0), sem(kind, l, 1), seq_at(d))

    def exchanged(src, dst, kind, l):
        wait_for(dst.at[pl.ds(0, NS - 1)], sem(kind, l, 1))
        wait_for(src.at[pl.ds(0, NS - 1)], sem(kind, l, 0))

    def to_x(make, kind, l):
        for k in (2, 1, 3):
            d = lax.rem(mx + k, NX)
            src, dst = make(d)
            send(src, dst, sem(kind, l, 0), sem(kind, l, 1), {"x": d})

    def from_x(ref, kind, l):
        wait_for(ref, sem(kind, l, 1))
        wait_for(ref, sem(kind, l, 0))

    def scatter_x(dst, kind, l):
        dst[pl.ds(mx, 1)] = R.pb[mine][None]
        to_x(
            lambda d: (R.pb.at[pl.ds(pl.multiple_of(d * 32, 32), 32)], dst.at[mx]), kind, l
        )

    def neighbour(src, dst, kind, l, step):
        other = me + step

        @pl.when((other >= 0) & (other < NS))
        def _():
            send(src, dst, sem(kind, l, 0), sem(kind, l, 1), seq_at(other))

    def neighbour_done(src, dst, kind, l, step):
        @pl.when((me + step >= 0) & (me + step < NS))
        def _():
            wait_for(src, sem(kind, l, 0))

        @pl.when((me - step >= 0) & (me - step < NS))
        def _():
            wait_for(dst, sem(kind, l, 1))

    def to_sibling(src, dst, kind, l):
        send(src, dst, sem(kind, l, 0), sem(kind, l, 1), {"c": 1 - ic})

    def weight(kind, l):
        src, dst = {
            K.WZ: (R.wzx_h.at[l, 0], R.wz.at[l, 0]),
            K.WX: (R.wzx_h.at[l, 1], R.wz.at[l, 1]),
            K.WB: (R.wbc_h.at[l], R.wb.at[l]),
            K.WD: (R.wdt_h.at[l], R.wd.at[l]),
            K.WO: (R.wout_h.at[l], R.wo.at[l]),
        }[kind]
        return pltpu.make_async_copy(src, dst, sem(kind, l, 0))

    for l in (0, 1):
        for kind in (K.WZ, K.WX, K.WB, K.WD, K.WO):
            weight(kind, l).start()

    barrier = pltpu.get_barrier_semaphore()

    @pl.loop(1, NS)
    def _(k):
        pl.semaphore_signal(
            barrier, inc=1, device_id=seq_at(lax.rem(me + k, NS)), device_id_type=MESH
        )

    for k in range(1, NX):
        pl.semaphore_signal(
            barrier, inc=1, device_id={"x": lax.rem(mx + k, NX)}, device_id_type=MESH
        )

    h_of = lax.broadcasted_iota(jnp.int32, (128, IL), 0)
    c_of = lax.broadcasted_iota(jnp.int32, (128, IL), 1)
    R.E[...] = jnp.where(c_of // 64 == h_of, 1.0, 0.0).astype(BF)
    c_of = lax.broadcasted_iota(jnp.int32, (IL, 128), 0)
    h_of = lax.broadcasted_iota(jnp.int32, (IL, 128), 1)
    R.Et[...] = jnp.where(c_of // 64 == h_of, 1.0, 0.0).astype(BF)
    row = lax.broadcasted_iota(jnp.int32, (TOK, TOK), 0)
    col = lax.broadcasted_iota(jnp.int32, (TOK, TOK), 1)
    R.tri[...] = jnp.where(row >= col, 1.0, 0.0).astype(BF)
    own = R.idc[HALO : HALO + TOK]
    for k in range(3):
        j = 3 - k
        R.mk[k] = jnp.where(R.idc[HALO - j : HALO + TOK - j] == own, 1.0, 0.0)
        R.mkb[k] = jnp.where(R.idc[HALO + j : HALO + TOK + j] == own, 1.0, 0.0)
    R.sm[...] = jnp.zeros((NS, 8, 128), F32)
    R.re[1, :, 640:] = jnp.zeros((TOK, 128), BF)
    for l in (0, 1):
        R.skE[l] = split_left(nn, R.hp[l], R.E[...], 3)

    @pl.when(me == 0)
    def _():
        R.nrm[:, 0:HALO] = jnp.zeros((2, HALO, D), BF)

    @pl.when(me == NS - 1)
    def _():
        R.dpre[:, TOK:] = jnp.zeros((2, 8, 1280), F32)

    lo = lax.broadcasted_iota(jnp.int32, (TOK, 128), 1) < 64

    def halves(pair):
        zero = jnp.zeros_like(pair)
        return jnp.where(lo, pair, zero), jnp.where(lo, zero, pair)

    def expand(src, dst):
        parts = pieces(src, 2)
        for j in range(4):
            c = slice(256 * j, 256 * j + 256)
            dst[:, c] = sum(nn(p, R.E[:, c]) for p in parts)

    def mixing(l, h):
        return (R.G[l] * R.L[l, h].astype(F32)).astype(BF)

    def normalize(u, l):
        r = lax.rsqrt(jnp.mean(u * u, axis=1, keepdims=True) + EPS)
        return (u * r * R.ng[l : l + 1, :]).astype(BF)

    def halo(l):
        return R.nrm.at[l, pl.ds(TOK, HALO)], R.nrm.at[l, pl.ds(0, HALO)]

    def project(l):
        weight(K.WZ, l).wait()

        @pl.loop(0, 4)
        def _(j):
            c = lanes(j, 256)
            R.z[l, :, c] = nn(R.nrm[l, HALO:], R.wz[l, 0, :, :, :, c].reshape(D, 256))

        neighbour_done(*halo(l), K.HA, l, 1)
        weight(K.WX, l).wait()

        @pl.loop(0, 4)
        def _(j):
            c = lanes(j, 256)
            R.v[l, :, c] = nn(R.nrm[l], R.wz[l, 1, :, :, :, c].reshape(D, 256))

        weight(K.WB, l).wait()
        R.v[l, :, IL:] = nn(R.nrm[l], R.wb[l])
        weight(K.WD, l).wait()
        wd = jnp.concatenate([R.wd[l], jnp.zeros((128 - HL, D), BF)], axis=0)
        R.dtr[l] = nt(R.nrm[l, HALO:], wd)

    def conv_sum(l, c):
        acc = R.ct[l, 4:5, c] + R.ct[l, 3:4, c] * R.v[l, HALO:, c]
        for k in range(3):
            acc = acc + (R.ct[l, k : k + 1, c] * R.mk[k]) * (
                R.v[l, HALO - 3 + k : HALO + TOK - 3 + k, c]
            )
        return acc

    def convolve(l):
        @pl.loop(0, 10)
        def _(j):
            c = lanes(j)
            acc = conv_sum(l, c)
            R.xbc[l, :, c] = (acc * sigmoid(acc)).astype(BF)

    def steps(l):
        raw = R.dtr[l] + R.hp[l, 0:1]
        dt = jnp.maximum(raw, 0.0) + jnp.log1p(jnp.exp(-jnp.abs(raw)))
        rate = -dt * jnp.exp(R.hp[l, 1:2])
        cum = split_right(nn, R.tri[...], rate, 3)
        R.dt[l] = dt
        R.rate[l] = rate
        R.cum[l] = cum
        flag = jnp.where(own == R.idc[HALO - 1 : HALO], 1.0, 0.0)
        ending = jnp.where(own == R.idc[HALO + TOK - 1 : HALO + TOK], 1.0, 0.0)
        entry = jnp.exp(cum) * flag
        R.entry[l] = entry
        R.wl[l] = jnp.exp(cum[TOK - 1 : TOK] - cum) * ending
        entry_t = entry.T
        heads = lax.broadcasted_iota(jnp.int32, (128, 128), 0) < HL
        R.dtot[l] = jnp.where(
            heads, jnp.broadcast_to(entry_t[:, TOK - 1 : TOK], (128, 128)), 0.0
        )

    def ssd(l):
        b_mat = R.xbc[l, :, IL : IL + ST]
        c_mat = R.xbc[l, :, IL + ST :]
        expand(R.dt[l], R.dtE)
        expand(R.wl[l], R.wlE)

        @pl.loop(0, 8)
        def _(j):
            c = lanes(j)
            xdt = (R.xbc[l, :, c].astype(F32) * R.dtE[:, c]).astype(BF)
            R.xdt[l, :, c] = xdt
            xw = (xdt.astype(F32) * R.wlE[:, c]).astype(BF)
            s = tn(xw, b_mat).astype(BF)
            R.S[l, c, :] = s
            R.sb[pl.ds(4 * j, 4), 0:32] = s.reshape(4, 32, 128)

        upper = lax.broadcasted_iota(jnp.int32, (16, 128), 0) < 8
        for h in range(HL):
            d = R.dtot[l, h : h + 1]
            hi = d.astype(BF).astype(F32)
            tile = jnp.where(
                upper, jnp.broadcast_to(hi, (16, 128)), jnp.broadcast_to(d - hi, (16, 128))
            ).astype(BF)
            R.sb[2 * h, 32:48] = tile
            R.sb[2 * h + 1, 32:48] = tile
        exchange(R.sb, R.rb.at[l], K.ST, l)
        R.G[l] = nt(c_mat, b_mat)
        keep = (own == R.idr[0:1]) & (row >= col)
        cum = R.cum[l]
        cum_t = cum.T
        for h in range(HL):
            spread = cum[:, h : h + 1] - cum_t[h : h + 1, :]
            ell = jnp.where(keep, jnp.exp(jnp.where(keep, spread, 0.0)), 0.0)
            R.L[l, h] = ell.astype(BF)

        @pl.loop(0, 8)
        def _(j):
            c = lanes(j)
            a, b = halves(R.xdt[l, :, c])
            R.y[l, :, c] = nn(mixing(l, 2 * j), a) + nn(mixing(l, 2 * j + 1), b)

    def scan_states(l):
        exchanged(R.sb, R.rb.at[l], K.ST, l)

        def step(b, state):
            R.eb[b] = state.reshape(32, 128).astype(BF)
            tile = R.rb[l, b, 32:48].astype(F32)
            d = tile[0:8] + tile[8:16]
            return state * d[None] + R.rb[l, b, 0:32].astype(F32).reshape(4, 8, 128)

        lax.fori_loop(0, NS, step, jnp.zeros((4, 8, 128), F32))
        exchange(R.eb, R.sin.at[l], K.EN, l)

    def gate(l):
        c_mat = R.xbc[l, :, IL + ST :]
        expand(R.entry[l], R.entE)
        exchanged(R.eb, R.sin.at[l], K.EN, l)

        def block(j, acc):
            c = lanes(j)
            sin = R.sin[l, pl.ds(4 * j, 4)].reshape(128, 128)
            xs = R.xbc[l, :, c].astype(F32)
            y = R.y[l, :, c] + nt(c_mat, sin) * R.entE[:, c] + R.skE[l, 2:3, c] * xs
            R.y[l, :, c] = y
            z = R.z[l, :, c]
            g = y * (z * sigmoid(z))
            gg = g * R.gg[l : l + 1, c]
            R.gs[:, c] = gg.astype(BF)
            if l == 0:
                return (acc[0] + g * g,)
            return (acc[0] + g * g, acc[1] + gg * R.ds[:, c])

        sums = lax.fori_loop(0, 8, block, (jnp.zeros((TOK, 128), F32),) * (l + 1))
        ones = jnp.ones((8, 128), BF)
        parts = [split_right(nt, ones, s, 2) for s in sums]
        if l == 0:
            R.sq[l] = parts[0]
        else:
            at = lax.broadcasted_iota(jnp.int32, (8, 128), 0)
            R.sq[l] = jnp.where(at == 0, parts[0], parts[1])
        R.sqx[l, pl.ds(mx, 1)] = R.sq[l][None]
        to_x(lambda d: (R.sq.at[l], R.sqx.at[l, mx]), K.SQ, l)

    def root(l):
        from_x(R.sqx.at[l, pl.ds(0, 3)], K.SQ, l)
        total = R.sqx[l, 0] + R.sqx[l, 1] + R.sqx[l, 2] + R.sqx[l, 3]
        q = lax.rsqrt(total[0:1] * (1.0 / INNER) + EPS)
        R.q[l] = jnp.broadcast_to(q, (128, 128)).T
        if l == 1:
            R.scol[...] = jnp.broadcast_to(total[1:2], (128, 128)).T

    def project_out(l):
        if l == 0:
            weight(K.WO, l).wait()

        @pl.loop(0, 8)
        def _(j):
            c = lanes(j, 256)
            R.pb[:, c] = nn(R.gs[...], R.wo[l, :, :, c].reshape(IL, 256)).astype(BF)

        scatter_x(R.rs.at[l], K.RS, l)

    def next_resid(l, before):
        from_x(R.rs.at[l, pl.ds(0, 3)], K.RS, l)
        total = sum(R.rs[l, k].astype(F32) for k in range(NX))
        if l == 0:
            R.br[...] = total
        return before + R.q[l, mine][:, 0:1] * total

    def gather_x(ref, kind, l):
        to_x(lambda d: (ref, ref), kind, l)

    def backward_gate(l):
        def block(j, acc):
            c = lanes(j)
            z, y = R.z[l, :, c], R.y[l, :, c]
            xs = R.xbc[l, :, c].astype(F32)
            sg = sigmoid(z)
            silu = z * sg
            g = y * silu
            ds, gain, q = R.ds[:, c], R.gg[l : l + 1, c], R.q[l]
            gq = g * q
            dg = ds * gain * q - gq * (q * q * R.scol[...] * (1.0 / INNER))
            dy = dg * silu
            R.ro[0, :, c] = (dg * y * (sg * (1.0 + z * (1.0 - sg)))).astype(BF)
            R.ro[1, :, c] = (gq * gain).astype(BF)
            R.sm[17 + l, pl.ds(j, 1)] = jnp.sum(ds * gq, axis=0, keepdims=True)
            R.dsk[:, c] = jnp.broadcast_to(
                jnp.sum(dy * xs, axis=0, keepdims=True), (8, 128)
            )
            sk = R.skE[l, 2:3, c]
            dyb = dy.astype(BF)
            dyf = dyb.astype(F32)
            R.dyb[:, c] = dyb
            R.dye[:, c] = (dyf * R.entE[:, c]).astype(BF)
            R.ds[:, c] = sk * dy
            direct = tn(R.dye[:, c], R.xbc[l, :, IL + ST :])
            R.sbb[pl.ds(4 * j, 4)] = direct.astype(BF).reshape(4, 32, 128)
            return acc + split_left(nn, dyf * (y - sk * xs), R.Et[c, :])

        R.rows[...] = lax.fori_loop(0, 8, block, jnp.zeros((TOK, 128), F32))
        exchange(R.sbb, R.rbb.at[l], K.SB, l)

    def backward_local(l):
        b_mat = R.xbc[l, :, IL : IL + ST]
        c_mat = R.xbc[l, :, IL + ST :]

        def block(j, dgram):
            c = lanes(j)
            a, b = halves(R.dyb[:, c])
            R.U[:, c] = tn(mixing(l, 2 * j), a) + tn(mixing(l, 2 * j + 1), b)
            xdt = R.xdt[l, :, c]
            return (
                dgram
                + nt(a, xdt) * R.L[l, 2 * j].astype(F32)
                + nt(b, xdt) * R.L[l, 2 * j + 1].astype(F32)
            )

        dgram = lax.fori_loop(0, 8, block, jnp.zeros((TOK, TOK), F32)).astype(BF)
        sin = R.sin[l].reshape(IL, ST)
        R.dbc[:, ST:] = nn(dgram, b_mat) + nn(R.dye[...], sin)
        R.dbc[:, 0:ST] = tn(dgram, c_mat)
        expand(R.dt[l], R.dtE)
        expand(R.wl[l], R.wlE)

    def scan_back(l):
        exchanged(R.sbb, R.rbb.at[l], K.SB, l)

        def step(i, state):
            b = NS - 1 - i
            R.eb[b] = state.reshape(32, 128).astype(BF)
            tile = R.rb[l, b, 32:48].astype(F32)
            d = tile[0:8] + tile[8:16]
            return state * d[None] + R.rbb[l, b].astype(F32).reshape(4, 8, 128)

        lax.fori_loop(0, NS, step, jnp.zeros((4, 8, 128), F32))
        exchange(R.eb, R.lam.at[l], K.EB, l)

    def backward_state(l):
        b_mat = R.xbc[l, :, IL : IL + ST]
        exchanged(R.eb, R.lam.at[l], K.EB, l)

        def block(j, carry):
            c = lanes(j)
            lam = R.lam[l, pl.ds(4 * j, 4)].reshape(128, 128)
            wl = R.wlE[:, c]
            ut = R.U[:, c] + wl * nt(b_mat, lam)
            xdt = R.xdt[l, :, c].astype(F32)
            R.ds[:, c] += R.dtE[:, c] * ut
            xw = (xdt * wl).astype(BF)
            lamf = lam.astype(F32)
            et = R.Et[c, :]
            sin = R.sin[l, pl.ds(4 * j, 4)].reshape(128, 128).astype(F32)
            return (
                carry[0] + nn(xw, lam),
                carry[1] + split_right(tn, et, lamf * R.S[l, c, :].astype(F32)),
                carry[2] + split_right(tn, et, lamf * sin),
                carry[3] + split_left(nn, xdt * ut, et),
                carry[4] + split_left(nn, R.xbc[l, :, c].astype(F32) * ut, et),
            )

        zero = jnp.zeros((128, 128), F32)
        db, ks, kd, less, ddt = lax.fori_loop(0, 8, block, (zero,) * 5)
        R.dbc[:, 0:ST] += db
        held = split_right(nt, jnp.ones((8, 128), BF), ks + R.dtot[l] * kd)
        last = lax.broadcasted_iota(jnp.int32, (TOK, 128), 0) == TOK - 1
        dcum = R.rows[...] - less + jnp.where(last, held[0:1], 0.0)
        drate = split_right(tn, R.tri[...], dcum, 3)
        ddt = ddt - drate * jnp.exp(R.hp[l, 1:2])
        ddtr = ddt * sigmoid(R.dtr[l] + R.hp[l, 0:1])
        R.re[0, :, 640:] = ddtr.astype(BF)
        at = 4 * l
        R.sm[19, at : at + 1] = jnp.sum(ddtr, axis=0, keepdims=True)
        R.sm[19, at + 1 : at + 2] = jnp.sum(drate * R.rate[l], axis=0, keepdims=True)
        R.sm[19, at + 2 : at + 3] = split_left(nn, R.dsk[...], R.Et[...])[0:1]

    def backward_conv(l):
        def block(c, dact):
            pre = conv_sum(l, c)
            sg = sigmoid(pre)
            R.dpre[l, 0:TOK, c] = dact * (sg * (1.0 + pre * (1.0 - sg)))

        @pl.loop(0, 8)
        def _(j):
            block(lanes(j), R.ds[:, lanes(j)])

        for j in range(2):
            block(pl.ds(IL + 128 * j, 128), R.dbc[:, 128 * j : 128 * j + 128])
        head, tail = R.dpre.at[l, pl.ds(0, 8)], R.dpre.at[l, pl.ds(TOK, 8)]
        neighbour(head, tail, K.DP, l, -1)

        def tap_sums(c):
            dpre = R.dpre[l, 0:TOK, c]
            out = []
            for k in range(3):
                shifted = R.v[l, HALO - 3 + k : HALO + TOK - 3 + k, c]
                out.append(jnp.sum(dpre * shifted * R.mk[k], axis=0, keepdims=True))
            out.append(jnp.sum(dpre * R.v[l, HALO:, c], axis=0, keepdims=True))
            return [*out, jnp.sum(dpre, axis=0, keepdims=True)]

        @pl.loop(0, 8)
        def _(j):
            for k, s in enumerate(tap_sums(lanes(j))):
                R.sm[7 + 5 * l + k, pl.ds(j, 1)] = s

        for j in range(2):
            for k, s in enumerate(tap_sums(pl.ds(IL + 128 * j, 128))):
                at = 12 * l + 2 * k + j
                R.sm[4 + at // 8, at % 8 : at % 8 + 1] = s
        neighbour_done(head, tail, K.DP, l, -1)

        def back(c):
            out = R.ct[l, 3:4, c] * R.dpre[l, 0:TOK, c]
            for k in range(3):
                out = out + (R.ct[l, k : k + 1, c] * R.mkb[k]) * (
                    R.dpre[l, 3 - k : TOK + 3 - k, c]
                )
            return out.astype(BF)

        for j in range(2):
            R.dbp[:, 128 * j : 128 * j + 128] = back(pl.ds(IL + 128 * j, 128))
        R.bx[l, pl.ds(mx, 1)] = R.dbp[...][None]
        to_x(lambda d: (R.dbp, R.bx.at[l, mx]), K.BX, l)

        @pl.loop(0, 8)
        def _(j):
            R.re[j // 4, :, lanes(lax.rem(j, 4))] = back(lanes(j))

    def sum_bc(l):
        from_x(R.bx.at[l, pl.ds(0, 3)], K.BX, l)
        both = sum(R.bx[l, k].astype(F32) for k in range(NX)).astype(BF)
        R.re[0, :, 512:640] = both[:, 0:128]
        R.re[1, :, 512:640] = both[:, 128:256]

    def backward_project(l):
        @pl.loop(0, 8)
        def _(j):
            rows = pl.ds(2 * lax.rem(j, 2), 2)
            wz = R.wz[l, 0, j // 2, rows].reshape(256, IL)
            wx = R.wz[l, 1, j // 2, rows].reshape(256, IL)
            c = lanes(j, 256)
            part = nt(R.ro[0], wz)
            part += nt(R.re[0, :, 0:512], wx[:, 0:512])
            part += nt(R.re[1, :, 0:512], wx[:, 512:])
            part += nt(R.dbp[...], R.wb[l, c, :])
            part += nn(R.re[0, :, 640 : 640 + HL], R.wd[l, :, c])
            R.pb[:, c] = part.astype(BF)

        scatter_x(R.rs.at[1 - l], K.RB, l)

    def backward_norm(l, above):
        from_x(R.rs.at[1 - l, pl.ds(0, 3)], K.RB, l)
        dn = sum(R.rs[1 - l, k].astype(F32) for k in range(NX))
        u = R.u[l]
        r = lax.rsqrt(jnp.mean(u * u, axis=1, keepdims=True) + EPS)
        gw = dn * R.ng[l : l + 1, :]
        gain = jnp.sum(dn * u * r, axis=0, keepdims=True)
        for i in range(16):
            R.sm[2 * l + i // 8, i % 8 : i % 8 + 1] = gain[:, 128 * i : 128 * i + 128]
        s = jnp.sum(gw * u, axis=1, keepdims=True) * (1.0 / D)
        return above + gw * r - u * (r * r * r * s)

    def back_scaled(l, src):
        @pl.loop(0, 4)
        def _(j):
            R.ds[:, lanes(j, 256)] = nt(src[...], R.wo[l, pl.ds(2 * j, 2)].reshape(256, D))

    def job(n):
        wide = n % 2 == 0
        half = (WIDE if wide else NARROW) // 2
        part = (R.part, R.wz.at[1, 0], R.part, R.wz.at[0, 0])[n]
        if n == 1:
            return part, half, lambda a, p: R.wz.at[
                1, 1, 2 * a + p // 2, :, :, lanes(lax.rem(p, 2), 512)
            ].at[:, :, pl.ds(0, half)]
        space = (R.wo.at[1], None, R.wo.at[1], R.wo.at[0])[n]
        return part, half, lambda a, p: space.at[
            pl.ds(4 * a, 4), :, pl.ds(pl.multiple_of(512 * p, 128), half)
        ]

    def jsem(n, kind, side):
        return R.jsem.at[n, kind, side]

    def job_rhs(n):
        src = R.ro if n % 2 == 0 else R.re
        dst = R.rsib.at[n % 2, :, pl.ds(0, WIDE if n % 2 == 0 else NARROW)]
        send(src.at[1 - ic], dst, jsem(n, J.RX, 0), jsem(n, J.RX, 1), {"c": 1 - ic})

    def job_product(n, l, lhs_own, lhs_sib):
        part, half, _ = job(n)
        src = R.ro if n % 2 == 0 else R.re

        @pl.loop(0, 4)
        def _(b):
            c = lanes(b, 512)
            left = jnp.concatenate([lhs_own(c), lhs_sib[:, c]], axis=0).T
            for k in range(2 * half // 256):
                w = slice(256 * k, 256 * k + 256)
                right = jnp.concatenate([src[ic, :, w], R.rsib[n % 2, :, w]], axis=0)
                part[b, :, :, w] = nn(left, right).astype(BF).reshape(4, 128, 256)

    def job_rhs_done(n):
        width = WIDE if n % 2 == 0 else NARROW
        ref = R.rsib.at[n % 2, :, pl.ds(0, width)]
        wait_for(ref, jsem(n, J.RX, 1))
        wait_for(ref, jsem(n, J.RX, 0))

    def job_multiply(n, l):
        job_rhs_done(n)

        def by_norm(c):
            return R.nrm[l, HALO:, c]

        if n % 2:
            job_product(n, l, by_norm, R.nsib)
            return
        branch = R.cot if l == 1 else R.dbr0

        @pl.when(ic == 0)
        def _():
            job_product(n, l, by_norm, R.nsib)

        @pl.when(ic == 1)
        def _():
            job_product(n, l, lambda c: branch[:, c], R.dsib)

    def job_send1(n):
        part, half, land = job(n)
        for k in (2, 1, 3):
            d = lax.rem(iy + k, 4)
            send(
                part.at[:, d, :, pl.ds(0, half)], land(0, iy),
                jsem(n, J.Y1, 0), jsem(n, J.Y1, 1), {"y": d},
            )
            d = lax.rem(iz + k, 4)
            send(
                part.at[d, :, :, pl.ds(half, half)], land(1, iz),
                jsem(n, J.Z1, 0), jsem(n, J.Z1, 1), {"z": d},
            )

    def job_sum1(n):
        part, half, land = job(n)
        three = part.at[pl.ds(0, 3), :, :, pl.ds(0, half)]
        wait_for(three, jsem(n, J.Y1, 1))
        wait_for(three, jsem(n, J.Y1, 0))
        slots = [land(0, lax.rem(iy + k, 4)) for k in (1, 2, 3)]

        @pl.loop(0, 4)
        def _(b):
            for w in range(0, half, 128):
                w = slice(w, w + 128)
                s = part[b, iy, :, w].astype(F32)
                for slot in slots:
                    s = s + slot[b, :, w].astype(F32)
                part[b, iy, :, w] = s.astype(BF)

        for k in (2, 1, 3):
            d = lax.rem(iz + k, 4)
            send(
                part.at[d, iy, :, pl.ds(0, half)], R.land.at[n, 0, iz, :, pl.ds(0, half)],
                jsem(n, J.Y2, 0), jsem(n, J.Y2, 1), {"z": d},
            )
        wait_for(three, jsem(n, J.Z1, 1))
        wait_for(three, jsem(n, J.Z1, 0))
        slots = [land(1, lax.rem(iz + k, 4)) for k in (1, 2, 3)]

        @pl.loop(0, 4)
        def _(b):
            for w in range(0, half, 128):
                at, w = slice(half + w, half + w + 128), slice(w, w + 128)
                s = part[iz, b, :, at].astype(F32)
                for slot in slots:
                    s = s + slot[b, :, w].astype(F32)
                part[iz, b, :, at] = s.astype(BF)

        for k in (2, 1, 3):
            d = lax.rem(iy + k, 4)
            send(
                part.at[iz, d, :, pl.ds(half, half)], R.land.at[n, 1, iy, :, pl.ds(0, half)],
                jsem(n, J.Z2, 0), jsem(n, J.Z2, 1), {"y": d},
            )

    def job_outputs(n, half_at, to_self):
        l = 1 - n // 2
        rows = pl.ds(pl.multiple_of(64 * half_at, 64), 64)
        kind = J.OWN if to_self else J.OUT

        def put(columns, dst):
            src = R.total.at[rows, columns]
            if to_self:
                pltpu.make_async_copy(src, dst, jsem(n, kind, 0)).start()
            else:
                send(src, dst, jsem(n, kind, 0), jsem(n, kind, 1), {"c": 1 - ic})

        @pl.when(ic == 0)
        def _():
            if n % 2 == 0:
                put(pl.ds(0, IL), R.zx_o.at[l, 0])
            else:
                put(pl.ds(0, 512), R.zx_o.at[l, 1, :, pl.ds(0, 512)])
                put(pl.ds(512, 128), R.bc_o.at[l, :, pl.ds(0, 128)])
                put(pl.ds(640, 128), R.dt_o.at[l])

        @pl.when(ic == 1)
        def _():
            if n % 2 == 0:
                put(pl.ds(0, IL), R.out_o.at[l])
            else:
                put(pl.ds(0, 512), R.zx_o.at[l, 1, :, pl.ds(512, 512)])
                put(pl.ds(512, 128), R.bc_o.at[l, :, pl.ds(128, 128)])

    def job_sum2(n):
        part, half, _ = job(n)
        three = R.land.at[n, 0, pl.ds(0, 3), :, pl.ds(0, half)]
        for kind in (J.Y2, J.Z2):
            wait_for(three, jsem(n, kind, 1))
            wait_for(three, jsem(n, kind, 0))
        for a, at in ((0, iz), (1, iy)):
            for w in range(0, half, 128):
                here, w = slice(a * half + w, a * half + w + 128), slice(w, w + 128)
                s = part[iz, iy, :, here].astype(F32)
                for k in (1, 2, 3):
                    s = s + R.land[n, a, lax.rem(at + k, 4), :, w].astype(F32)
                R.total[:, here] = s
        job_outputs(n, ic, True)
        job_outputs(n, 1 - ic, False)

    def job_done(n):
        def all_of(width, kind, side):
            wait_for(R.total.at[pl.ds(0, 64), pl.ds(0, width)], jsem(n, kind, side))

        if n % 2 == 0:
            for kind, side in ((J.OWN, 0), (J.OUT, 0), (J.OUT, 1)):
                all_of(IL, kind, side)
            return

        @pl.when(ic == 0)
        def _():
            for kind, side, width in ((J.OWN, 0, 768), (J.OUT, 0, 768), (J.OUT, 1, 640)):
                all_of(width, kind, side)

        @pl.when(ic == 1)
        def _():
            for kind, side, width in ((J.OWN, 0, 640), (J.OUT, 0, 640), (J.OUT, 1, 768)):
                all_of(width, kind, side)

    def sibling_done(ref, kind, l):
        wait_for(ref, sem(kind, l, 1))
        wait_for(ref, sem(kind, l, 0))

    def edge_out(i, dst, value):
        R.edge[i] = value.astype(BF)
        here = dst.at[mine]
        pltpu.make_async_copy(R.edge.at[i], here, sem(K.OWN, i, 0)).start()
        kind = (K.OH, K.GI)[i]
        to_x(lambda d: (R.edge.at[i], here), kind, 0)

    def edge_done(i, dst):
        wait_for(R.edge.at[i], sem(K.OWN, i, 0))
        from_x(dst.at[pl.ds(0, 96)], (K.OH, K.GI)[i], 0)

    @pl.loop(0, 4)
    def _(j):
        rows = pl.ds(pl.multiple_of(j * 32, 32), 32)
        at = pl.ds(pl.multiple_of(HALO + j * 32, 16), 32)
        R.nrm[0, at] = normalize(R.hid[rows].astype(F32), 0)

    R.u[0] = R.hid[mine].astype(F32)
    pl.semaphore_wait(barrier, NS - 1 + NX - 1)
    neighbour(*halo(0), K.HA, 0, 1)
    project(0)
    convolve(0)
    steps(0)
    ssd(0)
    scan_states(0)
    gate(0)
    project_out(0)
    root(0)
    R.u[1] = next_resid(0, R.u[0])
    at = pl.ds(pl.multiple_of(HALO + mx * 32, 16), 32)
    R.nrm[1, at] = normalize(R.u[1], 1)
    gather_x(R.nrm.at[1, at], K.AG, 1)
    from_x(R.nrm.at[1, pl.ds(HALO, 96)], K.AG, 1)
    neighbour(*halo(1), K.HA, 1, 1)
    project(1)
    convolve(1)
    steps(1)
    ssd(1)
    to_sibling(R.nrm.at[1, pl.ds(HALO, TOK)], R.nsib, K.NSIB, 1)
    to_sibling(R.cot, R.dsib, K.DSIB, 1)
    weight(K.WO, 1).wait()
    back_scaled(1, R.cot)
    scan_states(1)
    gate(1)
    project_out(1)
    root(1)
    backward_gate(1)
    job_rhs(0)
    edge_out(0, R.oh, next_resid(1, R.u[1]))
    backward_local(1)
    scan_back(1)
    sibling_done(R.nsib, K.NSIB, 1)
    sibling_done(R.dsib, K.DSIB, 1)
    job_multiply(0, 1)
    job_send1(0)
    backward_state(1)
    backward_conv(1)
    backward_project(1)
    sum_bc(1)
    job_rhs(1)
    job_multiply(1, 1)
    R.du[...] = backward_norm(1, R.cot[mine].astype(F32))
    R.dbr0[mine] = R.du[...].astype(BF)
    gather_x(R.dbr0.at[mine], K.AG, 0)
    s = jnp.sum(R.du[...].astype(BF).astype(F32) * R.br[...], axis=1, keepdims=True)
    R.scol[mine] = jnp.broadcast_to(s, (32, 128))
    gather_x(R.scol.at[mine], K.SC, 0)
    edge_done(0, R.oh)
    from_x(R.dbr0.at[pl.ds(0, 96)], K.AG, 0)
    back_scaled(0, R.dbr0)
    from_x(R.scol.at[pl.ds(0, 96)], K.SC, 0)
    expand(R.entry[0], R.entE)
    backward_gate(0)
    backward_local(0)
    job_sum1(0)
    scan_back(0)
    job_rhs(2)
    to_sibling(R.nrm.at[0, pl.ds(HALO, TOK)], R.nsib, K.NSIB, 0)
    to_sibling(R.dbr0, R.dsib, K.DSIB, 0)
    job_send1(1)
    job_sum2(0)
    sibling_done(R.nsib, K.NSIB, 0)
    sibling_done(R.dsib, K.DSIB, 0)
    job_multiply(2, 0)
    backward_state(0)
    job_send1(2)
    backward_conv(0)
    backward_project(0)
    sum_bc(0)
    job_rhs(3)
    job_multiply(3, 0)
    job_send1(3)
    edge_out(1, R.gi, backward_norm(0, R.du[...]))
    exchange(R.sm, R.smr, K.SM, 0)
    job_sum1(1)
    job_sum1(2)
    exchanged(R.sm, R.smr, K.SM, 0)
    mine_sum = sum(R.smr[k] for k in range(NS))
    R.smt[...] = mine_sum
    R.smx[pl.ds(mx, 1)] = mine_sum[None]
    to_x(lambda d: (R.smt, R.smx.at[mx]), K.SX, 0)
    job_done(0)
    job_sum2(1)
    from_x(R.smx.at[pl.ds(0, 3)], K.SX, 0)
    over_x = R.smx[0] + R.smx[1] + R.smx[2] + R.smx[3]
    R.smt[...] = jnp.where(me < 7, over_x, R.smt[...])
    R.sums[pl.ds(me, 1)] = R.smt[...][None]

    @pl.loop(1, NS)
    def _(k):
        send(
            R.smt, R.sums.at[me], sem(K.SG, 0, 0), sem(K.SG, 0, 1), seq_at(lax.rem(me + k, NS))
        )

    job_sum1(3)
    job_done(1)
    job_sum2(2)
    job_done(2)
    job_sum2(3)
    wait_for(R.sums.at[pl.ds(0, NS - 1)], sem(K.SG, 0, 1))
    wait_for(R.sums.at[pl.ds(0, NS - 1)], sem(K.SG, 0, 0))
    edge_done(1, R.gi)
    job_done(3)


def chain(*args):
    vmem = pl.BlockSpec(memory_space=pltpu.VMEM)
    held = pl.BlockSpec(memory_space=pl.ANY)
    return pl.pallas_call(
        chain_kernel,
        out_shape=[jax.ShapeDtypeStruct(s, t) for s, t, _ in OUT.values()],
        in_specs=[held if far else vmem for far in IN.values()],
        out_specs=[held if far else vmem for _, _, far in OUT.values()],
        scratch_shapes=[pltpu.VMEM(s, t) for s, t in SCRATCH.values()]
        + [pltpu.SemaphoreType.DMA((25, 2, 2)), pltpu.SemaphoreType.DMA((4, 7, 2))],
        compiler_params=pltpu.CompilerParams(
            collective_id=1, has_side_effects=True, vmem_limit_bytes=64 * 2**20
        ),
        name="chain",
    )(*args)


def local(
    hidden_in, cotangent, segment_ids, norm_gain, weight_zx, weight_bc, weight_dt, dt_bias, a_log,
    skip_scale, conv_x, conv_x_bias, conv_bc, conv_bc_bias, gate_gain, weight_out,
):
    me = position()
    padded = jnp.concatenate(
        [jnp.full((HALO,), -1, jnp.int32), segment_ids, jnp.full((HALO,), -2, jnp.int32)]
    )
    ids = lax.dynamic_slice_in_dim(padded, me * TOK, TOK + 2 * HALO)
    idc = jnp.broadcast_to(ids[:, None], (TOK + 2 * HALO, 128))
    idr = jnp.broadcast_to(ids[None, HALO : HALO + TOK], (8, 128))
    hp = jnp.pad(jnp.stack([dt_bias, a_log, skip_scale], axis=1), ((0, 0), (0, 5), (0, 128 - HL)))
    ct = jnp.concatenate(
        [
            jnp.concatenate([conv_x, conv_bc], axis=2),
            jnp.concatenate([conv_x_bias, conv_bc_bias], axis=1)[:, None],
            jnp.zeros((2, 3, 1280), F32),
        ],
        axis=1,
    )
    oh, gi, zx, out, bc, dt, sums = chain(
        hidden_in, cotangent, idc, idr, norm_gain, gate_gain, hp, ct,
        jnp.swapaxes(weight_zx, 1, 2).reshape(2, 2, 4, 4, 128, IL), weight_bc,
        jnp.swapaxes(weight_dt, 1, 2), weight_out.reshape(2, 8, 128, D),
    )
    norms = sums[0:4].reshape(2, D)
    by_bc = sums[4:7].reshape(2, 12, 128)[:, :10].reshape(2, 5, 256)
    by_x = sums[7:17].reshape(2, 5, IL)
    heads = sums[19].reshape(2, 4, 128)[:, :, :HL]
    return (
        oh, gi, lax.dynamic_slice_in_dim(norms, me * 64, 64, axis=1), jnp.swapaxes(zx, 1, 2), bc,
        dt[:, :, :HL], heads[:, 0], heads[:, 1], heads[:, 2], by_x[:, :4], by_x[:, 4],
        by_bc[:, :4], by_bc[:, 4], sums[17:19].reshape(2, IL), jnp.swapaxes(out, 1, 2),
    )


def solution(mesh):
    finer = Mesh(mesh.devices.reshape(4, 4, 2, 4), ("z", "y", "c", "x"))
    in_specs = (
        P(SEQ, None), P(SEQ, None), P(), P(), P(None, None, None, "x"), P(), P(None, None, "x"),
        P(None, "x"), P(None, "x"), P(None, "x"), P(None, None, "x"), P(None, "x"), P(), P(),
        P(None, "x"), P(None, "x", None),
    )
    out_specs = (
        P(SEQ, None), P(SEQ, None), P(None, SEQ), P(None, SEQ, None, "x"), P(None, SEQ, None),
        P(None, SEQ, "x"), P(None, "x"), P(None, "x"), P(None, "x"), P(None, None, "x"),
        P(None, "x"), P(), P(), P(None, "x"), P(None, "x", SEQ),
    )
    return jax.shard_map(local, mesh=finer, in_specs=in_specs, out_specs=out_specs, check_vma=False)
```

time: 1120 us -> 282 us (0.25); the launches traced: 1100 us -> 281 us
  waiting for transfers between devices: 453 us -> 0 us
  Pallas kernels: 0 us -> 239 us
  starting transfers between devices: 139 us -> 0 us
  other arithmetic: 142 us -> 3.52 us
  matrix products: 122 us -> 0 us
  blocking collectives: 120 us -> 0 us
  local copies, waits for them, and re-layouts: 109 us -> 38.4 us
  between operations: 18 us -> 0.71 us
    all_gather x12 -> x0, waiting for transfers between devices: 261 us -> none  [the longest x2 141 us: backward_layer(): lax.all_gather(grad_columns, SEQ, axis=0, tiled=True)]
    pallas_call x0 -> x1, Pallas kernels: none -> 239 us  [chain(): pl.pallas_call(chain_kernel, out_shape=[jax.ShapeDtypeStruct(s, t) for s,...]
    all_to_all x28 -> x0, waiting for transfers between devices: 191 us -> none  [the longest x26 188 us: copy_for_each(): lax.all_to_all(jnp.broadcast_to(array[None], (devices, *array.shape)), ax...]
    dot_general x54 -> x0, matrix products: 122 us -> none  [the longest x2 22.3 us: backward_layer(): jnp.einsum('tr,tc->rc', feature_slab, lax.all_gather(grad_columns, SEQ, a...]
    all_to_all x28 -> x0, starting transfers between devices: 118 us -> none  [the longest x26 109 us: copy_for_each(): lax.all_to_all(jnp.broadcast_to(array[None], (devices, *array.shape)), ax...]
    all_gather x14 -> x0, blocking collectives: 79.7 us -> none  [the longest x8 43.2 us: entering_2(): lax.all_gather(part.astype(kind), axis)]
    reduce_sum x45 -> x0, other arithmetic: 45.6 us -> none  [the longest x22 17.8 us: of_everyone(): return jnp.sum(everything, axis=0)]
    all_to_all x4 -> x0, blocking collectives: 40.4 us -> none  [copy_for_each(): lax.all_to_all(jnp.broadcast_to(array[None], (devices, *array.shape)), ax...]
  transfers between devices with their start and end apart: 48 -> 0, of which waited for: 36 -> 0; matrix products, arithmetic and copies ran while one was open for 22% -> 0% of each run, Pallas kernels for 0% -> 0%
where the time goes in v1:
time: 282 us; the launch traced here: 281 us
  Pallas kernels  239 us (85%)
  local copies, waits for them, and re-layouts  38.4 us (14%)
  other arithmetic  3.52 us (1%)
    pallas_call x1, Pallas kernels, chain(): pl.pallas_call(chain_kernel, out_shape=[jax.ShapeDtypeStruct(s, t) for s,...  239 us
    transpose x1, local copies, waits for them, and re-layouts, local(): jnp.swapaxes(weight_zx, 1, 2).reshape(2, 2, 4, 4, 128, IL)  16.4 us
    unnamed x10, local copies, waits for them, and re-layouts  14.2 us

profile of v1, /device:TPU:1, one launch (start us, length us, event | category | flops | bytes accessed | tf_op | source)
XLA Modules:
  0.0 281.2 jit_solution(4040631473113285305)
XLA Ops:
  0.7 1.3 select_maximum_fusion.refs_6_
  2.1 0.7 pad_maximum_fusion
  2.8 0.8 concatenate.12
  3.8 0.6 broadcast_in_dim.9.refs_3_
  4.4 1.5 maximum_maximum_fusion.refs_7_
  5.8 0.7 broadcast_in_dim.8.refs_2_
  6.6 16.4 %copy.45 = bf16[2,2,2048,1024]{3,2,1,0:T(8,128)(2,1)} copy(bf16[2,2,2048,1024]{3,1,2,0:T(2,128)(2,1)} %bitcast.39) | data formatting | bytes 33554432 | tf_op jit(solution)/shard_map/transpose | solution.py:1025
  23.0 238.6 %chain.1 = (bf16[128,2048]{1,0:T(8,128)(2,1)}, bf16[128,2048]{1,0:T(8,128)(2,1)}, f32[2,2,64,1024]{3,2,1,0:T(8,128)}, f32[2,64,1024]{2,1,0:T(8,128)}, f32[2,64,2...) custom-call(bf16[128,2048]{1,0:T(8,128)(2,1)} %refs_0_.1, bf16[128,2048]{1,0:T(8,128)(2,1)} %refs_1_.1, ...), custom_call_target="tpu_custom_call" | custom-call | tf_op jit(solution)/shard_map/chain/pallas_call | solution.py:989
  261.6 0.7 slice.52
  262.8 0.7 slice_bitcast_fusion
  263.5 0.6 copy.60
  264.1 0.7 slice.59
  264.9 0.6 slice.70
  266.0 1.5 copy.50
  267.6 0.7 slice.50
  268.3 0.8 slice.56
  269.1 0.6 constant_dynamic-slice_fusion
  269.7 0.6 slice.67
  270.4 0.6 copy.61
  271.0 3.0 %copy.49 = f32[2,64,2,1024]{3,2,1,0:T(2,128)} copy(f32[2,64,2,1024]{3,1,2,0:T(8,128)} %bitcast.41) | data formatting | bytes 2097152
  274.0 1.9 copy.67
  275.8 1.9 copy.68
  277.7 1.6 copy.69
  279.3 1.9 copy.70
  (15 shorter events, 1.4 us)

commit v2 on v1

v2 whole, which is shorter than its diff:
```python
import types

import jax
import jax.numpy as jnp
from jax import lax
from jax.experimental import pallas as pl
from jax.experimental.pallas import tpu as pltpu
from jax.sharding import Mesh
from jax.sharding import PartitionSpec as P

D = 2048
INNER = 4096
IL = 1024
TOK = 128
ST = 128
HL = 16
NS = 32
NX = 4
HALO = 16
SEQ = ("z", "y", "c")
EPS = 1e-05
F32 = jnp.float32
BF = jnp.bfloat16
MESH = pl.DeviceIdType.MESH
WIDE, NARROW = 1024, 768


def dot(a, b, ca, cb):
    return lax.dot_general(a, b, (((ca,), (cb,)), ((), ())), preferred_element_type=F32)


def nn(a, b):
    return dot(a, b, 1, 0)


def nt(a, b):
    return dot(a, b, 1, 1)


def tn(a, b):
    return dot(a, b, 0, 0)


def pieces(a, count):
    out = []
    for _ in range(count):
        p = a.astype(BF)
        out.append(p)
        a = a - p.astype(F32)
    return out


def split_left(f, a, exact, count=2):
    return sum(f(p, exact) for p in pieces(a, count))


def split_right(f, exact, a, count=2):
    return sum(f(exact, p) for p in pieces(a, count))


def sigmoid(v):
    return 1.0 / (1.0 + jnp.exp(-v))


def seq_at(s):
    return {"z": s // 8, "y": lax.rem(s // 2, 4), "c": lax.rem(s, 2)}


def position():
    return lax.axis_index("z") * 8 + lax.axis_index("y") * 2 + lax.axis_index("c")


def lanes(j, width=128, base=0):
    return pl.ds(pl.multiple_of(base + j * width, 128), width)


def wait_for(ref, sem):
    pltpu.make_async_copy(ref, ref, sem).wait()


IN = dict(
    hid=1, cot=0, seg=0, ng=0, gg=0, dtb=0, alog=0, skip=0, cx=0, cxb=0, cbc=0, cbcb=0,
    wzx_h=1, wbc_h=1, wdt_h=1, wout_h=1,
)
OUT = dict(
    oh=((TOK, D), BF, 1),
    gi=((TOK, D), BF, 1),
    zx_o=((2, 64, 2, IL), F32, 1),
    out_o=((2, 64, IL), F32, 1),
    bc_o=((2, 64, 256), F32, 1),
    dt_o=((2, 64, 128), F32, 1),
    sums=((NS, 8, 128), F32, 0),
)
SCRATCH = dict(
    wz=((2, D, 2, IL), BF),
    wb=((2, D, 256), BF),
    wd=((2, HL, D), BF),
    wo=((2, 8, 128, D), BF),
    nrm=((2, HALO + TOK, D), BF),
    dbr0=((TOK, D), BF),
    z=((2, TOK, IL), F32),
    v=((2, HALO + TOK, 1280), F32),
    xbc=((2, TOK, 1280), BF),
    xdt=((2, TOK, IL), BF),
    L=((2, HL, TOK, TOK), BF),
    G=((2, TOK, TOK), F32),
    y=((2, TOK, IL), F32),
    S=((2, IL, ST), BF),
    dtr=((2, TOK, 128), F32),
    dt=((2, TOK, 128), F32),
    rate=((2, TOK, 128), F32),
    cum=((2, TOK, 128), F32),
    entry=((2, TOK, 128), F32),
    wl=((2, TOK, 128), F32),
    dtot=((2, 128, 128), F32),
    q=((2, TOK, 128), F32),
    skE=((2, 8, IL), F32),
    u=((2, 32, D), F32),
    br=((32, D), F32),
    mk=((3, TOK, 128), F32),
    mkb=((3, TOK, 128), F32),
    E=((128, IL), BF),
    Et=((IL, 128), BF),
    tri=((TOK, TOK), BF),
    sb=((NS, 48, 128), BF),
    rb=((2, NS, 48, 128), BF),
    eb=((NS, 32, 128), BF),
    sin=((2, NS, 32, 128), BF),
    rbb=((NS, 32, 128), BF),
    lam=((NS, 32, 128), BF),
    sq=((2, 8, 128), F32),
    sqx=((2, NX, 8, 128), F32),
    pb=((TOK, D), BF),
    rs=((2, NX, 32, D), BF),
    ds=((TOK, IL), F32),
    dbc=((TOK, 256), F32),
    dyb=((TOK, IL), BF),
    dye=((TOK, IL), BF),
    U=((8, TOK, 128), F32),
    rows=((TOK, 128), F32),
    dsk=((8, IL), F32),
    dpre=((2, TOK + 8, 1280), F32),
    scol=((TOK, 128), F32),
    du=((32, D), F32),
    edge=((2, 32, D), BF),
    dbp=((TOK, 256), BF),
    bx=((NX, TOK, 256), BF),
    ro=((2, TOK, WIDE), BF),
    re=((2, TOK, NARROW), BF),
    idc=((TOK + 2 * HALO, 128), F32),
    hp=((2, 8, 128), F32),
    ct=((2, 8, 1280), F32),
    nx=((17, 16, 2 * D), BF),
    pick=((128, 512), BF),
    nbt=((4, 4, 128, 128), BF),
    dbt=((4, 4, 128, 128), BF),
    nl=((2, 2, 4, 128, 1024), BF),
    dl=((2, 2, 4, 128, 1024), BF),
    land=((3, 2, 4, 8, 16, 512), BF),
    total=((2, 128, WIDE), F32),
    x2t=((IL, 256), BF),
    sm=((NS, 8, 128), F32),
    smr=((NS, 8, 128), F32),
    smt=((8, 128), F32),
    smx=((NX, 8, 128), F32),
)


class K:
    (
        HID, WZ, WB, WD, WO, ST, EN, SB, EB, SQ, RS, RB, AG, HA, DP, SC, OH, GI, NY, NZ, DY, DZ,
        FY, FZ, BX, SM, SX, SG, OWN,
    ) = range(29)


class J:
    Y1, Z1, Y2, Z2, OUT, OWN = range(6)


def chain_kernel(*refs):
    R = types.SimpleNamespace(**dict(zip([*IN, *OUT, *SCRATCH, "sem", "jsem"], refs)))
    iz, iy, ic, mx = (lax.axis_index(a) for a in ("z", "y", "c", "x"))
    R.sbb = R.sb.at[:, pl.ds(0, 32)]
    me = position()
    mine = pl.ds(pl.multiple_of(mx * 32, 32), 32)

    def sem(kind, l, side):
        return R.sem.at[kind, l, side]

    def send(src, dst, s, r, to):
        pltpu.make_async_remote_copy(
            src, dst, s, r, device_id=to, device_id_type=MESH
        ).start()

    def exchange(src, dst, kind, l):
        dst[pl.ds(me, 1)] = src[pl.ds(me, 1)]

        @pl.loop(1, NS)
        def _(k):
            d = lax.rem(me + k, NS)
            send(src.at[d], dst.at[me], sem(kind, l, 0), sem(kind, l, 1), seq_at(d))

    def exchanged(src, dst, kind, l):
        wait_for(dst.at[pl.ds(0, NS - 1)], sem(kind, l, 1))
        wait_for(src.at[pl.ds(0, NS - 1)], sem(kind, l, 0))

    def to_x(make, kind, l):
        for k in (2, 1, 3):
            d = lax.rem(mx + k, NX)
            src, dst = make(d)
            send(src, dst, sem(kind, l, 0), sem(kind, l, 1), {"x": d})

    def from_x(ref, kind, l):
        wait_for(ref, sem(kind, l, 1))
        wait_for(ref, sem(kind, l, 0))

    def scatter_x(dst, kind, l, piece):
        c = pl.ds(512 * piece, 512)
        dst[mx, :, c] = R.pb[mine, c]
        to_x(
            lambda d: (
                R.pb.at[pl.ds(pl.multiple_of(d * 32, 32), 32), c], dst.at[mx, :, c]
            ),
            kind, l,
        )

    def neighbour(src, dst, kind, l, step):
        other = me + step

        @pl.when((other >= 0) & (other < NS))
        def _():
            send(src, dst, sem(kind, l, 0), sem(kind, l, 1), seq_at(other))

    def neighbour_done(src, dst, kind, l, step):
        @pl.when((me + step >= 0) & (me + step < NS))
        def _():
            wait_for(src, sem(kind, l, 0))

        @pl.when((me - step >= 0) & (me - step < NS))
        def _():
            wait_for(dst, sem(kind, l, 1))

    def weight(kind, l):
        src, dst = {
            K.WZ: (R.wzx_h.at[l], R.wz.at[l]),
            K.WB: (R.wbc_h.at[l], R.wb.at[l]),
            K.WD: (R.wdt_h.at[l], R.wd.at[l]),
            K.WO: (R.wout_h.at[l], R.wo.at[l]),
        }[kind]
        return pltpu.make_async_copy(src, dst, sem(kind, l, 0))

    resid_in = pltpu.make_async_copy(R.hid, R.pb, sem(K.HID, 0, 0))
    resid_in.start()
    for l in (0, 1):
        for kind in (K.WZ, K.WB, K.WD, K.WO):
            weight(kind, l).start()

    barrier = pltpu.get_barrier_semaphore()

    @pl.loop(1, NS)
    def _(k):
        pl.semaphore_signal(
            barrier, inc=1, device_id=seq_at(lax.rem(me + k, NS)), device_id_type=MESH
        )

    for k in range(1, NX):
        pl.semaphore_signal(
            barrier, inc=1, device_id={"x": lax.rem(mx + k, NX)}, device_id_type=MESH
        )

    last_x = mx == NX - 1

    @pl.when(last_x & (me < NS - 1))
    def _():
        for k in range(NX - 1):
            pl.semaphore_signal(
                barrier, inc=1, device_id={**seq_at(me + 1), "x": k}, device_id_type=MESH
            )

    @pl.when((mx < NX - 1) & (me > 0))
    def _():
        pl.semaphore_signal(
            barrier, inc=1, device_id={**seq_at(me - 1), "x": NX - 1}, device_id_type=MESH
        )

    def everyone_is_here():
        has_next, has_prev = 1 - (me + 1) // NS, (me + NS - 1) // NS
        at_end = mx // (NX - 1)
        pl.semaphore_wait(
            barrier, NS - 1 + NX - 1 + at_end * has_next * (NX - 1) + (1 - at_end) * has_prev
        )

    def ids_of(s):
        return jnp.broadcast_to(R.seg[pl.ds(s, 1)].astype(F32), (128, 128))

    R.idc[HALO : HALO + TOK] = ids_of(me).T
    R.idc[0:HALO] = jnp.where(me == 0, -1.0, ids_of(lax.rem(me + NS - 1, NS)).T[TOK - HALO :])
    R.idc[HALO + TOK :] = jnp.where(me == NS - 1, -2.0, ids_of(lax.rem(me + 1, NS)).T[0:HALO])
    R.hp[...] = jnp.zeros((2, 8, 128), F32)
    R.ct[...] = jnp.zeros((2, 8, 1280), F32)
    for l in (0, 1):
        for i, ref in enumerate((R.dtb, R.alog, R.skip)):
            R.hp[l, i : i + 1, 0:HL] = ref[l : l + 1]
        R.ct[l, 0:4, 0:IL] = R.cx[l]
        R.ct[l, 0:4, IL:] = R.cbc[l]
        R.ct[l, 4:5, 0:IL] = R.cxb[l : l + 1]
        R.ct[l, 4:5, IL:] = R.cbcb[l : l + 1]
    r_of = lax.broadcasted_iota(jnp.int32, (128, 512), 0)
    c_of = lax.broadcasted_iota(jnp.int32, (128, 512), 1)
    R.pick[...] = jnp.where((c_of == 2 * r_of) | (c_of == 2 * r_of + 257), 1.0, 0.0).astype(BF)
    h_of = lax.broadcasted_iota(jnp.int32, (128, IL), 0)
    c_of = lax.broadcasted_iota(jnp.int32, (128, IL), 1)
    R.E[...] = jnp.where(c_of // 64 == h_of, 1.0, 0.0).astype(BF)
    c_of = lax.broadcasted_iota(jnp.int32, (IL, 128), 0)
    h_of = lax.broadcasted_iota(jnp.int32, (IL, 128), 1)
    R.Et[...] = jnp.where(c_of // 64 == h_of, 1.0, 0.0).astype(BF)
    row = lax.broadcasted_iota(jnp.int32, (TOK, TOK), 0)
    col = lax.broadcasted_iota(jnp.int32, (TOK, TOK), 1)
    R.tri[...] = jnp.where(row >= col, 1.0, 0.0).astype(BF)
    own = R.idc[HALO : HALO + TOK]
    for k in range(3):
        j = 3 - k
        R.mk[k] = jnp.where(R.idc[HALO - j : HALO + TOK - j] == own, 1.0, 0.0)
        R.mkb[k] = jnp.where(R.idc[HALO + j : HALO + TOK + j] == own, 1.0, 0.0)
    R.sm[...] = jnp.zeros((NS, 8, 128), F32)
    R.re[1, :, 640:] = jnp.zeros((TOK, 128), BF)
    for l in (0, 1):
        R.skE[l] = split_left(nn, R.hp[l], R.E[...], 3)

    @pl.when(me == 0)
    def _():
        R.nrm[:, 0:HALO] = jnp.zeros((2, HALO, D), BF)

    @pl.when(me == NS - 1)
    def _():
        R.dpre[:, TOK:] = jnp.zeros((2, 8, 1280), F32)

    lo = lax.broadcasted_iota(jnp.int32, (TOK, 128), 1) < 64

    def halves(pair):
        zero = jnp.zeros_like(pair)
        return jnp.where(lo, pair, zero), jnp.where(lo, zero, pair)

    def expanded(parts, c):
        return sum(nn(p, R.E[:, c]) for p in parts)

    def mixing(l, h):
        return (R.G[l] * R.L[l, h].astype(F32)).astype(BF)

    def normalize(u, l):
        r = lax.rsqrt(jnp.mean(u * u, axis=1, keepdims=True) + EPS)
        return (u * r * R.ng[l : l + 1, :]).astype(BF)

    def halo(l):
        return R.nrm.at[l, pl.ds(TOK, HALO)], R.nrm.at[l, pl.ds(0, HALO)]

    def spread_rows(l, first, rows, at):
        @pl.loop(0, 16, unroll=8)
        def _(j):
            n = R.nrm[l, first : first + rows, lanes(j)]
            if at is None:
                both = nn(n, R.pick[...]).astype(BF)
                R.nx[0:8, :, lanes(j, 256)] = both[:, 0:256].reshape(8, 16, 256)
                R.nx[9:, :, lanes(j, 256)] = both[:, 256:].reshape(8, 16, 256)
            else:
                R.nx[at // 16, :, lanes(j, 256)] = nn(n, R.pick[:, 256:]).astype(BF)

    def halo_done(l):
        if l == 0:
            neighbour_done(*halo(0), K.HA, 0, 1)
            return

        @pl.when(last_x & (me < NS - 1))
        def _():
            four = R.nrm.at[1, pl.ds(0, 4 * HALO)]
            wait_for(four, sem(K.HA, 1, 0))

        @pl.when(me > 0)
        def _():
            wait_for(halo(1)[1], sem(K.HA, 1, 1))

    def project(l):
        spread_rows(l, HALO, TOK, None)
        halo_done(l)
        spread_rows(l, 0, HALO, TOK)
        weight(K.WZ, l).wait()

        @pl.loop(0, 4)
        def _(j):
            c = lanes(j, 256)
            both = nn(R.nx[...].reshape(17 * 16, 2 * D), R.wz[l, :, :, c].reshape(2 * D, 256))
            R.z[l, :, c] = both[0:TOK]
            R.v[l, :, c] = both[TOK:]

        weight(K.WB, l).wait()
        R.v[l, :, IL:] = nn(R.nrm[l], R.wb[l])
        weight(K.WD, l).wait()
        wd = jnp.concatenate([R.wd[l], jnp.zeros((128 - HL, D), BF)], axis=0)
        R.dtr[l] = nt(R.nrm[l, HALO:], wd)

    def conv_sum(l, c):
        acc = R.ct[l, 4:5, c] + R.ct[l, 3:4, c] * R.v[l, HALO:, c]
        for k in range(3):
            acc = acc + (R.ct[l, k : k + 1, c] * R.mk[k]) * (
                R.v[l, HALO - 3 + k : HALO + TOK - 3 + k, c]
            )
        return acc

    def convolve(l):
        @pl.loop(0, 10, unroll=2)
        def _(j):
            c = lanes(j)
            acc = conv_sum(l, c)
            R.xbc[l, :, c] = (acc * sigmoid(acc)).astype(BF)

    def steps(l):
        raw = R.dtr[l] + R.hp[l, 0:1]
        dt = jnp.maximum(raw, 0.0) + jnp.log1p(jnp.exp(-jnp.abs(raw)))
        rate = -dt * jnp.exp(R.hp[l, 1:2])
        cum = split_right(nn, R.tri[...], rate, 3)
        R.dt[l] = dt
        R.rate[l] = rate
        R.cum[l] = cum
        flag = jnp.where(own == R.idc[HALO - 1 : HALO], 1.0, 0.0)
        ending = jnp.where(own == R.idc[HALO + TOK - 1 : HALO + TOK], 1.0, 0.0)
        entry = jnp.exp(cum) * flag
        R.entry[l] = entry
        R.wl[l] = jnp.exp(cum[TOK - 1 : TOK] - cum) * ending
        entry_t = entry.T
        heads = lax.broadcasted_iota(jnp.int32, (128, 128), 0) < HL
        R.dtot[l] = jnp.where(
            heads, jnp.broadcast_to(entry_t[:, TOK - 1 : TOK], (128, 128)), 0.0
        )

    def ssd(l):
        b_mat = R.xbc[l, :, IL : IL + ST]
        c_mat = R.xbc[l, :, IL + ST :]
        dt, wl = pieces(R.dt[l], 2), pieces(R.wl[l], 2)

        @pl.loop(0, 8, unroll=4)
        def _(j):
            c = lanes(j)
            xdt = (R.xbc[l, :, c].astype(F32) * expanded(dt, c)).astype(BF)
            R.xdt[l, :, c] = xdt
            xw = (xdt.astype(F32) * expanded(wl, c)).astype(BF)
            s = tn(xw, b_mat).astype(BF)
            R.S[l, c, :] = s
            R.sb[pl.ds(4 * j, 4), 0:32] = s.reshape(4, 32, 128)

        upper = lax.broadcasted_iota(jnp.int32, (16, 128), 0) < 8
        for h in range(HL):
            d = R.dtot[l, h : h + 1]
            hi = d.astype(BF).astype(F32)
            tile = jnp.where(
                upper, jnp.broadcast_to(hi, (16, 128)), jnp.broadcast_to(d - hi, (16, 128))
            ).astype(BF)
            R.sb[2 * h, 32:48] = tile
            R.sb[2 * h + 1, 32:48] = tile
        exchange(R.sb, R.rb.at[l], K.ST, l)
        R.G[l] = nt(c_mat, b_mat)
        keep = (own == ids_of(me)[0:1]) & (row >= col)
        cum = R.cum[l]
        cum_t = cum.T
        for h in range(HL):
            spread = cum[:, h : h + 1] - cum_t[h : h + 1, :]
            ell = jnp.where(keep, jnp.exp(jnp.where(keep, spread, 0.0)), 0.0)
            R.L[l, h] = ell.astype(BF)

        @pl.loop(0, 8, unroll=4)
        def _(j):
            c = lanes(j)
            a, b = halves(R.xdt[l, :, c])
            R.y[l, :, c] = nn(mixing(l, 2 * j), a) + nn(mixing(l, 2 * j + 1), b)

    def scan_states(l):
        exchanged(R.sb, R.rb.at[l], K.ST, l)

        def step(b, state):
            R.eb[b] = state.reshape(32, 128).astype(BF)
            tile = R.rb[l, b, 32:48].astype(F32)
            d = tile[0:8] + tile[8:16]
            return state * d[None] + R.rb[l, b, 0:32].astype(F32).reshape(4, 8, 128)

        lax.fori_loop(0, NS, step, jnp.zeros((4, 8, 128), F32), unroll=8)
        exchange(R.eb, R.sin.at[l], K.EN, l)

    def gate(l):
        c_mat = R.xbc[l, :, IL + ST :]
        entry = pieces(R.entry[l], 2)
        exchanged(R.eb, R.sin.at[l], K.EN, l)

        def block(j, acc):
            c = lanes(j)
            sin = R.sin[l, pl.ds(4 * j, 4)].reshape(128, 128)
            xs = R.xbc[l, :, c].astype(F32)
            y = R.y[l, :, c] + nt(c_mat, sin) * expanded(entry, c) + R.skE[l, 2:3, c] * xs
            R.y[l, :, c] = y
            z = R.z[l, :, c]
            g = y * (z * sigmoid(z))
            gg = g * R.gg[l : l + 1, c]
            R.dye[:, c] = gg.astype(BF)
            if l == 0:
                return (acc[0] + g * g,)
            return (acc[0] + g * g, acc[1] + gg * R.ds[:, c])

        sums = lax.fori_loop(0, 8, block, (jnp.zeros((TOK, 128), F32),) * (l + 1), unroll=4)
        ones = jnp.ones((8, 128), BF)
        parts = [split_right(nt, ones, s, 2) for s in sums]
        if l == 0:
            R.sq[l] = parts[0]
        else:
            at = lax.broadcasted_iota(jnp.int32, (8, 128), 0)
            R.sq[l] = jnp.where(at == 0, parts[0], parts[1])
        R.sqx[l, pl.ds(mx, 1)] = R.sq[l][None]
        to_x(lambda d: (R.sq.at[l], R.sqx.at[l, mx]), K.SQ, l)

    def root(l):
        from_x(R.sqx.at[l, pl.ds(0, 3)], K.SQ, l)
        total = R.sqx[l, 0] + R.sqx[l, 1] + R.sqx[l, 2] + R.sqx[l, 3]
        q = lax.rsqrt(total[0:1] * (1.0 / INNER) + EPS)
        R.q[l] = jnp.broadcast_to(q, (128, 128)).T
        if l == 1:
            R.scol[...] = jnp.broadcast_to(total[1:2], (128, 128)).T

    def project_out(l):
        if l == 0:
            weight(K.WO, l).wait()

        for p in range(4):
            for j in range(2):
                c = slice(512 * p + 256 * j, 512 * p + 256 * j + 256)
                R.pb[:, c] = nn(R.dye[...], R.wo[l, :, :, c].reshape(IL, 256)).astype(BF)
            scatter_x(R.rs.at[l], K.RS, l, p)

    def next_resid(l, before):
        from_x(R.rs.at[l, pl.ds(0, 3)], K.RS, l)
        total = sum(R.rs[l, k].astype(F32) for k in range(NX))
        if l == 0:
            R.br[...] = total
        return before + R.q[l, mine][:, 0:1] * total

    def gather_x(ref, kind, l):
        to_x(lambda d: (ref, ref), kind, l)

    def backward_gate(l):
        entry = pieces(R.entry[l], 2)

        def block(j, acc):
            c = lanes(j)
            z, y = R.z[l, :, c], R.y[l, :, c]
            xs = R.xbc[l, :, c].astype(F32)
            sg = sigmoid(z)
            silu = z * sg
            g = y * silu
            ds, gain, q = R.ds[:, c], R.gg[l : l + 1, c], R.q[l]
            gq = g * q
            dg = ds * gain * q - gq * (q * q * R.scol[...] * (1.0 / INNER))
            dy = dg * silu
            R.ro[0, :, c] = (dg * y * (sg * (1.0 + z * (1.0 - sg)))).astype(BF)
            R.ro[1, :, c] = (gq * gain).astype(BF)
            R.sm[17 + l, pl.ds(j, 1)] = jnp.sum(ds * gq, axis=0, keepdims=True)
            R.dsk[:, c] = jnp.broadcast_to(
                jnp.sum(dy * xs, axis=0, keepdims=True), (8, 128)
            )
            sk = R.skE[l, 2:3, c]
            dyb = dy.astype(BF)
            dyf = dyb.astype(F32)
            R.dyb[:, c] = dyb
            R.dye[:, c] = (dyf * expanded(entry, c)).astype(BF)
            R.ds[:, c] = sk * dy
            direct = tn(R.dye[:, c], R.xbc[l, :, IL + ST :])
            R.sbb[pl.ds(4 * j, 4)] = direct.astype(BF).reshape(4, 32, 128)
            return acc + split_left(nn, dyf * (y - sk * xs), R.Et[c, :])

        R.rows[...] = lax.fori_loop(0, 8, block, jnp.zeros((TOK, 128), F32), unroll=4)
        exchange(R.sbb, R.rbb, K.SB, l)

    def backward_local(l):
        b_mat = R.xbc[l, :, IL : IL + ST]
        c_mat = R.xbc[l, :, IL + ST :]

        def block(j, dgram):
            c = lanes(j)
            a, b = halves(R.dyb[:, c])
            R.U[j] = tn(mixing(l, 2 * j), a) + tn(mixing(l, 2 * j + 1), b)
            xdt = R.xdt[l, :, c]
            return (
                dgram
                + nt(a, xdt) * R.L[l, 2 * j].astype(F32)
                + nt(b, xdt) * R.L[l, 2 * j + 1].astype(F32)
            )

        dgram = lax.fori_loop(0, 8, block, jnp.zeros((TOK, TOK), F32), unroll=4).astype(BF)
        sin = R.sin[l].reshape(IL, ST)
        R.dbc[:, ST:] = nn(dgram, b_mat) + nn(R.dye[...], sin)
        R.dbc[:, 0:ST] = tn(dgram, c_mat)

    def scan_back(l):
        exchanged(R.sbb, R.rbb, K.SB, l)

        def step(i, state):
            b = NS - 1 - i
            R.eb[b] = state.reshape(32, 128).astype(BF)
            tile = R.rb[l, b, 32:48].astype(F32)
            d = tile[0:8] + tile[8:16]
            return state * d[None] + R.rbb[b].astype(F32).reshape(4, 8, 128)

        lax.fori_loop(0, NS, step, jnp.zeros((4, 8, 128), F32), unroll=8)
        exchange(R.eb, R.lam, K.EB, l)

    def backward_state(l):
        b_mat = R.xbc[l, :, IL : IL + ST]
        dt, wls = pieces(R.dt[l], 2), pieces(R.wl[l], 2)
        exchanged(R.eb, R.lam, K.EB, l)

        def block(j, carry):
            c = lanes(j)
            lam = R.lam[pl.ds(4 * j, 4)].reshape(128, 128)
            wl = expanded(wls, c)
            ut = R.U[j] + wl * nt(b_mat, lam)
            xdt = R.xdt[l, :, c].astype(F32)
            R.ds[:, c] += expanded(dt, c) * ut
            xw = (xdt * wl).astype(BF)
            lamf = lam.astype(F32)
            et = R.Et[c, :]
            sin = R.sin[l, pl.ds(4 * j, 4)].reshape(128, 128).astype(F32)
            return (
                carry[0] + nn(xw, lam),
                carry[1] + split_right(tn, et, lamf * R.S[l, c, :].astype(F32)),
                carry[2] + split_right(tn, et, lamf * sin),
                carry[3] + split_left(nn, xdt * ut, et),
                carry[4] + split_left(nn, R.xbc[l, :, c].astype(F32) * ut, et),
            )

        zero = jnp.zeros((128, 128), F32)
        db, ks, kd, less, ddt = lax.fori_loop(0, 8, block, (zero,) * 5, unroll=4)
        R.dbc[:, 0:ST] += db
        held = split_right(nt, jnp.ones((8, 128), BF), ks + R.dtot[l] * kd)
        last = lax.broadcasted_iota(jnp.int32, (TOK, 128), 0) == TOK - 1
        dcum = R.rows[...] - less + jnp.where(last, held[0:1], 0.0)
        drate = split_right(tn, R.tri[...], dcum, 3)
        ddt = ddt - drate * jnp.exp(R.hp[l, 1:2])
        ddtr = ddt * sigmoid(R.dtr[l] + R.hp[l, 0:1])
        R.re[0, :, 640:] = ddtr.astype(BF)
        at = 4 * l
        R.sm[19, at : at + 1] = jnp.sum(ddtr, axis=0, keepdims=True)
        R.sm[19, at + 1 : at + 2] = jnp.sum(drate * R.rate[l], axis=0, keepdims=True)
        R.sm[19, at + 2 : at + 3] = split_left(nn, R.dsk[...], R.Et[...])[0:1]

    def backward_conv(l):
        def block(c, dact):
            pre = conv_sum(l, c)
            sg = sigmoid(pre)
            R.dpre[l, 0:TOK, c] = dact * (sg * (1.0 + pre * (1.0 - sg)))

        @pl.loop(0, 8, unroll=2)
        def _(j):
            block(lanes(j), R.ds[:, lanes(j)])

        for j in range(2):
            block(pl.ds(IL + 128 * j, 128), R.dbc[:, 128 * j : 128 * j + 128])
        head, tail = R.dpre.at[l, pl.ds(0, 8)], R.dpre.at[l, pl.ds(TOK, 8)]
        neighbour(head, tail, K.DP, l, -1)

        def tap_sums(c):
            dpre = R.dpre[l, 0:TOK, c]
            out = []
            for k in range(3):
                shifted = R.v[l, HALO - 3 + k : HALO + TOK - 3 + k, c]
                out.append(jnp.sum(dpre * shifted * R.mk[k], axis=0, keepdims=True))
            out.append(jnp.sum(dpre * R.v[l, HALO:, c], axis=0, keepdims=True))
            return [*out, jnp.sum(dpre, axis=0, keepdims=True)]

        @pl.loop(0, 8, unroll=2)
        def _(j):
            for k, s in enumerate(tap_sums(lanes(j))):
                R.sm[7 + 5 * l + k, pl.ds(j, 1)] = s

        for j in range(2):
            for k, s in enumerate(tap_sums(pl.ds(IL + 128 * j, 128))):
                at = 12 * l + 2 * k + j
                R.sm[4 + at // 8, at % 8 : at % 8 + 1] = s
        neighbour_done(head, tail, K.DP, l, -1)
        job_share(2 - 2 * l, (1,))

        def back(c):
            out = R.ct[l, 3:4, c] * R.dpre[l, 0:TOK, c]
            for k in range(3):
                out = out + (R.ct[l, k : k + 1, c] * R.mkb[k]) * (
                    R.dpre[l, 3 - k : TOK + 3 - k, c]
                )
            return out.astype(BF)

        for j in range(2):
            R.dbp[:, 128 * j : 128 * j + 128] = back(pl.ds(IL + 128 * j, 128))
        R.bx[pl.ds(mx, 1)] = R.dbp[...][None]
        to_x(lambda d: (R.dbp, R.bx.at[mx]), K.BX, l)

        @pl.loop(0, 8, unroll=2)
        def _(j):
            R.re[j // 4, :, lanes(lax.rem(j, 4))] = back(lanes(j))

    def sum_bc(l):
        from_x(R.bx.at[pl.ds(0, 3)], K.BX, l)
        both = sum(R.bx[k].astype(F32) for k in range(NX)).astype(BF)
        R.re[0, :, 512:640] = both[:, 0:128]
        R.re[1, :, 512:640] = both[:, 128:256]

    def backward_project(l):
        R.x2t[:, 0:TOK] = R.ro[0].T
        for k in range(2):
            R.x2t[512 * k : 512 * k + 512, TOK:] = R.re[k, :, 0:512].T
        dbp_t = R.dbp[...].T
        dt_t = R.re[0, :, 640:].T[0:HL]
        for p in range(4):
            for j in range(2 * p, 2 * p + 2):
                rows = slice(256 * j, 256 * j + 256)
                both = nn(R.wz[l, rows].reshape(512, IL), R.x2t[...])
                part = nn(R.wb[l, rows, :], dbp_t) + tn(R.wd[l, :, rows], dt_t)
                for k in range(2):
                    buf = R.U.reshape(2, 512, 128).at[k]
                    buf[...] = both[:, TOK * k : TOK * k + TOK]
                    part += buf[pl.ds(k, 256, stride=2), :]
                R.pb[:, rows] = part.T.astype(BF)
            scatter_x(R.rs.at[1 - l], K.RB, l, p)

    def backward_norm(l, above):
        from_x(R.rs.at[1 - l, pl.ds(0, 3)], K.RB, l)
        dn = sum(R.rs[1 - l, k].astype(F32) for k in range(NX))
        u = R.u[l]
        r = lax.rsqrt(jnp.mean(u * u, axis=1, keepdims=True) + EPS)
        gw = dn * R.ng[l : l + 1, :]
        gain = jnp.sum(dn * u * r, axis=0, keepdims=True)
        for i in range(16):
            R.sm[2 * l + i // 8, i % 8 : i % 8 + 1] = gain[:, 128 * i : 128 * i + 128]
        s = jnp.sum(gw * u, axis=1, keepdims=True) * (1.0 / D)
        return above + gw * r - u * (r * r * r * s)

    def back_scaled(l, src):
        @pl.loop(0, 4, unroll=2)
        def _(j):
            R.ds[:, lanes(j, 256)] = nt(src[...], R.wo[l, pl.ds(2 * j, 2)].reshape(256, D))

    def transposed(src, dst):
        @pl.loop(0, 16, unroll=8)
        def _(j):
            dst[j // 4, lax.rem(j, 4)] = src(lanes(j)).T

    AXES = (("y", iy), ("z", iz))

    def left_block(src, a, p):
        return src.at[:, p] if a == 0 else src.at[p]

    def share_left(l):
        for a, (axis, at) in enumerate(AXES):
            slot = lanes(2 * at + ic)
            dst = R.nl.at[l, a, :, :, slot]
            for k in (2, 1, 3):
                p = lax.rem(at + k, 4)
                kind = (K.NY, K.NZ)[a]
                send(left_block(R.nbt, a, p), dst, sem(kind, l, 0), sem(kind, l, 1), {axis: p})
            dst[...] = left_block(R.nbt, a, at)[...]

    def pass_left(l):
        for a, (axis, at) in enumerate(AXES):
            kind, three = (K.NY, K.NZ)[a], R.nl.at[l, a, :, :, pl.ds(0, 384)]
            wait_for(three, sem(kind, l, 1))
            wait_for(three, sem(kind, l, 0))
            for k in range(4):
                ref = R.nl.at[l, a, :, :, lanes(2 * k + ic)]
                kind = (K.FY, K.FZ)[a]
                send(ref, ref, sem(kind, l, 0), sem(kind, l, 1), {"c": 1 - ic})

    def left_done(l):
        for a in range(2):
            four = R.nl.at[l, a, :, :, pl.ds(0, 512)]
            wait_for(four, sem((K.FY, K.FZ)[a], l, 1))
            wait_for(four, sem((K.FY, K.FZ)[a], l, 0))

    def share_branch(l):
        for a, (axis, at) in enumerate(AXES):
            slot = lanes(2 * at + ic)
            dst, kind = R.dl.at[l, a, :, :, slot], (K.DY, K.DZ)[a]

            def remote(p, dst=dst, kind=kind, axis=axis, a=a):
                send(
                    left_block(R.dbt, a, p), dst, sem(kind, l, 0), sem(kind, l, 1),
                    {axis: p, "c": 1},
                )

            for k in (2, 1, 3):
                remote(lax.rem(at + k, 4))

            @pl.when(ic == 0)
            def _(remote=remote, at=at):
                remote(at)

            @pl.when(ic == 1)
            def _(dst=dst, a=a, at=at):
                dst[...] = left_block(R.dbt, a, at)[...]

    def branch_done(l):
        for a in range(2):

            def count(blocks, side, a=a):
                ref = R.dl.at[l, a, :, :, pl.ds(0, 128 * blocks)]
                wait_for(ref, sem((K.DY, K.DZ)[a], l, side))

            @pl.when(ic == 1)
            def _(count=count):
                count(7, 1)
                count(3, 0)

            @pl.when(ic == 0)
            def _(count=count):
                count(4, 0)

    def job(n):
        wide = n % 2 == 0
        half = (WIDE if wide else NARROW) // 2

        def land(a, slot):
            return R.wo.at[1, slot, :, pl.ds((0 if wide else 1024) + 512 * a, half)]

        return half, land, R.ro if wide else R.re

    def prod(n, a, block, width):
        at = pl.multiple_of(512 * (4 * a + block), 512)
        return R.nx.at[pl.ds(8 * (n % 2), 8), :, pl.ds(at, width)]

    def land2(n):
        return R.land.at[(0, 1, 0, 2)[n]]

    def jsem(n, kind, side):
        return R.jsem.at[n, kind, side]

    def job_share(n, cores, axes=(0, 1)):
        half, land, src = job(n)
        for a in axes:
            axis, at = AXES[a]
            kind = (J.Y1, J.Z1)[a]
            slot = 2 * at + ic
            c = pl.ds(half * a, half)
            for k in (2, 1, 3, 0):
                p = lax.rem(at + k, 4)
                for core in cores:
                    to = {axis: p, "c": core}

                    def remote(core=core, c=c, a=a, slot=slot, kind=kind, to=to):
                        send(
                            src.at[core, :, c], land(a, slot), jsem(n, kind, 0), jsem(n, kind, 1),
                            to,
                        )

                    if k:
                        remote()
                    else:
                        pl.when(ic != core)(remote)

                        @pl.when(ic == core)
                        def _(core=core, c=c, a=a, slot=slot):
                            land(a, slot)[...] = src[core, :, c]

    def job_multiply(n, l):
        half, land, _ = job(n)
        seven = R.wo.at[1, pl.ds(0, 7), :, pl.ds(0, half)]
        for kind in (J.Y1, J.Z1):
            wait_for(seven, jsem(n, kind, 1))
            wait_for(seven, jsem(n, kind, 0))

        def product(left):
            for a in range(2):
                for w in range(0, half, 256):
                    width = min(256, half - w)
                    at = (0 if n % 2 == 0 else 1024) + 512 * a + w
                    right = R.wo[1, :, :, at : at + width].reshape(1024, width)
                    out = nn(left[a].reshape(512, 1024), right)
                    out = out.astype(BF).reshape(4, 8, 16, width)
                    for b in range(4):
                        at = 512 * (4 * a + b) + w
                        R.nx[8 * (n % 2) : 8 * (n % 2) + 8, :, at : at + width] = out[b]

        if n % 2:
            product(R.nl.at[l])
            return

        @pl.when(ic == 0)
        def _():
            product(R.nl.at[l])

        @pl.when(ic == 1)
        def _():
            product(R.dl.at[l])

    def job_reduce(n):
        half, _, _ = job(n)
        c = pl.ds(0, half)
        for k in (2, 1, 3):
            for a, at, axis, kind in ((0, iz, "z", J.Z2), (1, iy, "y", J.Y2)):
                p = lax.rem(at + k, 4)
                send(
                    prod(n, a, p, half), land2(n).at[a, at, :, :, c], jsem(n, kind, 0),
                    jsem(n, kind, 1), {axis: p},
                )

    def job_outputs(n, half_at, to_self):
        l = 1 - n // 2
        rows = pl.ds(pl.multiple_of(64 * half_at, 64), 64)
        kind = J.OWN if to_self else J.OUT

        def put(columns, dst):
            src = R.total.at[n % 2, rows, columns]
            if to_self:
                pltpu.make_async_copy(src, dst, jsem(n, kind, 0)).start()
            else:
                send(src, dst, jsem(n, kind, 0), jsem(n, kind, 1), {"c": 1 - ic})

        @pl.when(ic == 0)
        def _():
            if n % 2 == 0:
                put(pl.ds(0, IL), R.zx_o.at[l, :, 0])
            else:
                put(pl.ds(0, 512), R.zx_o.at[l, :, 1, pl.ds(0, 512)])
                put(pl.ds(512, 128), R.bc_o.at[l, :, pl.ds(0, 128)])
                put(pl.ds(640, 128), R.dt_o.at[l])

        @pl.when(ic == 1)
        def _():
            if n % 2 == 0:
                put(pl.ds(0, IL), R.out_o.at[l])
            else:
                put(pl.ds(0, 512), R.zx_o.at[l, :, 1, pl.ds(512, 512)])
                put(pl.ds(512, 128), R.bc_o.at[l, :, pl.ds(128, 128)])

    def job_sum2(n):
        half, _, _ = job(n)
        three = land2(n).at[0, pl.ds(0, 3), :, :, pl.ds(0, half)]
        for kind in (J.Y2, J.Z2):
            wait_for(three, jsem(n, kind, 1))
            wait_for(three, jsem(n, kind, 0))
        for a, at in ((0, iz), (1, iy)):
            for w in range(0, half, 128):
                here, w = slice(a * half + w, a * half + w + 128), slice(w, w + 128)
                first = pl.multiple_of(512 * (4 * a + at) + w.start, 128)
                s = R.nx[8 * (n % 2) : 8 * (n % 2) + 8, :, pl.ds(first, 128)].astype(F32)
                for k in (1, 2, 3):
                    s = s + land2(n)[a, lax.rem(at + k, 4), :, :, w].astype(F32)
                R.total[n % 2, :, here] = s.reshape(128, 128)
        job_outputs(n, ic, True)
        job_outputs(n, 1 - ic, False)

    def job_done(n):
        def all_of(width, kind, side):
            wait_for(R.total.at[0, pl.ds(0, 64), pl.ds(0, width)], jsem(n, kind, side))

        if n % 2 == 0:
            for kind, side in ((J.OWN, 0), (J.OUT, 0), (J.OUT, 1)):
                all_of(IL, kind, side)
            return

        @pl.when(ic == 0)
        def _():
            for kind, side, width in ((J.OWN, 0, 768), (J.OUT, 0, 768), (J.OUT, 1, 640)):
                all_of(width, kind, side)

        @pl.when(ic == 1)
        def _():
            for kind, side, width in ((J.OWN, 0, 640), (J.OUT, 0, 640), (J.OUT, 1, 768)):
                all_of(width, kind, side)

    def edge_out(i, dst, value):
        R.edge[i] = value.astype(BF)
        here = dst.at[mine]
        pltpu.make_async_copy(R.edge.at[i], here, sem(K.OWN, i, 0)).start()
        kind = (K.OH, K.GI)[i]
        to_x(lambda d: (R.edge.at[i], here), kind, 0)

    def edge_done(i, dst):
        wait_for(R.edge.at[i], sem(K.OWN, i, 0))
        from_x(dst.at[pl.ds(0, 96)], (K.OH, K.GI)[i], 0)

    resid_in.wait()

    @pl.loop(0, 4)
    def _(j):
        rows = pl.ds(pl.multiple_of(j * 32, 32), 32)
        at = pl.ds(pl.multiple_of(HALO + j * 32, 16), 32)
        R.nrm[0, at] = normalize(R.pb[rows].astype(F32), 0)

    R.u[0] = R.pb[mine].astype(F32)
    everyone_is_here()
    neighbour(*halo(0), K.HA, 0, 1)
    project(0)
    convolve(0)
    steps(0)
    ssd(0)
    transposed(lambda c: R.nrm[0, HALO:, c], R.nbt)
    transposed(lambda c: R.cot[:, c], R.dbt)
    scan_states(0)
    gate(0)
    share_left(0)
    share_branch(1)
    project_out(0)
    root(0)
    R.u[1] = next_resid(0, R.u[0])
    at = pl.ds(pl.multiple_of(HALO + mx * 32, 16), 32)
    R.nrm[1, at] = normalize(R.u[1], 1)

    gather_x(R.nrm.at[1, at], K.AG, 1)

    @pl.when(last_x & (me < NS - 1))
    def _():
        src, dst = halo(1)
        for k in range(NX):
            send(src, dst, sem(K.HA, 1, 0), sem(K.HA, 1, 1), {**seq_at(me + 1), "x": k})

    from_x(R.nrm.at[1, pl.ds(HALO, 96)], K.AG, 1)
    project(1)
    convolve(1)
    steps(1)
    ssd(1)
    pass_left(0)
    transposed(lambda c: R.nrm[1, HALO:, c], R.nbt)
    weight(K.WO, 1).wait()
    back_scaled(1, R.cot)
    scan_states(1)
    gate(1)
    share_left(1)
    project_out(1)
    root(1)
    backward_gate(1)
    backward_local(1)
    scan_back(1)
    job_share(0, (0,))
    edge_out(0, R.oh, next_resid(1, R.u[1]))
    pass_left(1)
    left_done(0)
    branch_done(1)
    backward_state(1)
    backward_conv(1)
    job_share(1, (0, 1), (0,))
    backward_project(1)
    sum_bc(1)
    job_share(1, (0, 1), (1,))
    R.du[...] = backward_norm(1, R.cot[mine].astype(F32))
    R.dbr0[mine] = R.du[...].astype(BF)
    gather_x(R.dbr0.at[mine], K.AG, 0)
    s = jnp.sum(R.du[...].astype(BF).astype(F32) * R.br[...], axis=1, keepdims=True)
    R.scol[mine] = jnp.broadcast_to(s, (32, 128))
    gather_x(R.scol.at[mine], K.SC, 0)
    edge_done(0, R.oh)
    left_done(1)
    job_multiply(0, 1)
    job_reduce(0)
    from_x(R.dbr0.at[pl.ds(0, 96)], K.AG, 0)
    transposed(lambda c: R.dbr0[:, c], R.dbt)
    share_branch(0)
    back_scaled(0, R.dbr0)
    from_x(R.scol.at[pl.ds(0, 96)], K.SC, 0)
    backward_gate(0)
    job_multiply(1, 1)
    job_reduce(1)
    backward_local(0)
    job_sum2(0)
    scan_back(0)
    job_share(2, (0,))
    job_sum2(1)
    backward_state(0)
    backward_conv(0)
    job_share(3, (0, 1), (0,))
    backward_project(0)
    sum_bc(0)
    job_share(3, (0, 1), (1,))
    branch_done(0)
    job_multiply(2, 0)
    job_reduce(2)
    edge_out(1, R.gi, backward_norm(0, R.du[...]))
    exchange(R.sm, R.smr, K.SM, 0)
    job_done(0)
    job_multiply(3, 0)
    job_reduce(3)
    exchanged(R.sm, R.smr, K.SM, 0)
    mine_sum = sum(R.smr[k] for k in range(NS))
    R.smt[...] = mine_sum
    R.smx[pl.ds(mx, 1)] = mine_sum[None]
    to_x(lambda d: (R.smt, R.smx.at[mx]), K.SX, 0)
    job_sum2(2)
    from_x(R.smx.at[pl.ds(0, 3)], K.SX, 0)
    over_x = R.smx[0] + R.smx[1] + R.smx[2] + R.smx[3]
    R.smt[...] = jnp.where(me < 7, over_x, R.smt[...])
    R.sums[pl.ds(me, 1)] = R.smt[...][None]

    @pl.loop(1, NS)
    def _(k):
        send(
            R.smt, R.sums.at[me], sem(K.SG, 0, 0), sem(K.SG, 0, 1), seq_at(lax.rem(me + k, NS))
        )

    job_done(1)
    job_sum2(3)
    edge_done(1, R.gi)
    job_done(2)
    wait_for(R.sums.at[pl.ds(0, NS - 1)], sem(K.SG, 0, 1))
    wait_for(R.sums.at[pl.ds(0, NS - 1)], sem(K.SG, 0, 0))
    job_done(3)


def chain(*args):
    vmem = pl.BlockSpec(memory_space=pltpu.VMEM)
    held = pl.BlockSpec(memory_space=pl.ANY)
    return pl.pallas_call(
        chain_kernel,
        out_shape=[jax.ShapeDtypeStruct(s, t) for s, t, _ in OUT.values()],
        in_specs=[held if far else vmem for far in IN.values()],
        out_specs=[held if far else vmem for _, _, far in OUT.values()],
        scratch_shapes=[pltpu.VMEM(s, t) for s, t in SCRATCH.values()]
        + [pltpu.SemaphoreType.DMA((29, 2, 2)), pltpu.SemaphoreType.DMA((4, 6, 2))],
        compiler_params=pltpu.CompilerParams(
            collective_id=1, has_side_effects=True, vmem_limit_bytes=64 * 2**20
        ),
        name="chain",
    )(*args)


def finish_kernel(
    oh, gi, zx, out, bc, dt, sums,
    oh_o, gi_o, norm_o, zx_o, bc_o, dt_o, bias_o, alog_o, skip_o, cx_o, cxb_o, cbc_o, cbcb_o,
    gate_o, out_o, sem,
):
    me = position()
    moves = [(oh, oh_o), (gi, gi_o), (out, out_o), (bc, bc_o), (zx, zx_o)]
    copies = [pltpu.make_async_copy(a, b, sem.at[i]) for i, (a, b) in enumerate(moves)]
    for c in copies:
        c.start()
    for l in range(2):
        block = me // 2
        row = sums[2 * l + block // 8, pl.ds(lax.rem(block, 8), 1)]
        norm_o[l : l + 1] = jnp.where(lax.rem(me, 2) == 0, row[:, 0:64], row[:, 64:])
        dt_o[l] = dt[l].T[0:HL]
        for i, ref in enumerate((bias_o, alog_o, skip_o)):
            ref[l : l + 1] = sums[19, 4 * l + i : 4 * l + i + 1, 0:HL]
        for j in range(8):
            c = slice(128 * j, 128 * j + 128)
            for k in range(4):
                cx_o[l, k : k + 1, c] = sums[7 + 5 * l + k, j : j + 1]
            cxb_o[l : l + 1, c] = sums[11 + 5 * l, j : j + 1]
            gate_o[l : l + 1, c] = sums[17 + l, j : j + 1]
        for j in range(2):
            c = slice(128 * j, 128 * j + 128)
            for k in range(5):
                at = 12 * l + 2 * k + j
                v = sums[4 + at // 8, at % 8 : at % 8 + 1]
                if k < 4:
                    cbc_o[l, k : k + 1, c] = v
                else:
                    cbcb_o[l : l + 1, c] = v
    for c in copies:
        c.wait()


def finish(*args):
    vmem = pl.BlockSpec(memory_space=pltpu.VMEM)
    held = pl.BlockSpec(memory_space=pl.ANY)
    shapes = [
        ((TOK, D), BF, 0), ((TOK, D), BF, 0), ((2, 64), F32, 0), ((2, 64, 2, IL), F32, 0),
        ((2, 64, 256), F32, 0), ((2, HL, 64), F32, 0), ((2, HL), F32, 0), ((2, HL), F32, 0),
        ((2, HL), F32, 0), ((2, 4, IL), F32, 0), ((2, IL), F32, 0), ((2, 4, 256), F32, 0),
        ((2, 256), F32, 0), ((2, IL), F32, 0), ((2, 64, IL), F32, 0),
    ]
    return pl.pallas_call(
        finish_kernel,
        out_shape=[jax.ShapeDtypeStruct(s, t) for s, t, _ in shapes],
        in_specs=[held] * 5 + [vmem] * 2,
        out_specs=[held if far else vmem for _, _, far in shapes],
        scratch_shapes=[pltpu.SemaphoreType.DMA((8,))],
        name="finish",
    )(*args)


def local(
    hidden_in, cotangent, segment_ids, norm_gain, weight_zx, weight_bc, weight_dt, dt_bias, a_log,
    skip_scale, conv_x, conv_x_bias, conv_bc, conv_bc_bias, gate_gain, weight_out,
):
    done = finish(
        *chain(
            hidden_in, cotangent, segment_ids.reshape(NS, TOK), norm_gain, gate_gain, dt_bias,
            a_log, skip_scale, conv_x, conv_x_bias, conv_bc, conv_bc_bias, weight_zx, weight_bc,
            jnp.swapaxes(weight_dt, 1, 2), weight_out.reshape(2, 8, 128, D),
        )
    )
    return (*done[:5], jnp.swapaxes(done[5], 1, 2), *done[6:14], jnp.swapaxes(done[14], 1, 2))


def solution(mesh):
    finer = Mesh(mesh.devices.reshape(4, 4, 2, 4), ("z", "y", "c", "x"))
    in_specs = (
        P(SEQ, None), P(SEQ, None), P(), P(), P(None, None, None, "x"), P(), P(None, None, "x"),
        P(None, "x"), P(None, "x"), P(None, "x"), P(None, None, "x"), P(None, "x"), P(), P(),
        P(None, "x"), P(None, "x", None),
    )
    out_specs = (
        P(SEQ, None), P(SEQ, None), P(None, SEQ), P(None, SEQ, None, "x"), P(None, SEQ, None),
        P(None, SEQ, "x"), P(None, "x"), P(None, "x"), P(None, "x"), P(None, None, "x"),
        P(None, "x"), P(), P(), P(None, "x"), P(None, "x", SEQ),
    )
    return jax.shard_map(local, mesh=finer, in_specs=in_specs, out_specs=out_specs, check_vma=False)
```

time: 282 us -> 189 us (0.67)
  Pallas kernels: 239 us -> 188 us
  local copies, waits for them, and re-layouts: 38.4 us -> 0 us
  other arithmetic: 3.52 us -> 0 us
    pallas_call x1, Pallas kernels: 239 us -> 183 us  [chain(): pl.pallas_call(chain_kernel, out_shape=[jax.ShapeDtypeStruct(s, t) for s,...]
    transpose x1 -> x0, local copies, waits for them, and re-layouts: 16.4 us -> none  [local(): jnp.swapaxes(weight_zx, 1, 2).reshape(2, 2, 4, 4, 128, IL)]
    unnamed x10 -> x0, local copies, waits for them, and re-layouts: 14.2 us -> none
    slice x10 -> x0, local copies, waits for them, and re-layouts: 4.77 us -> none  [the longest x1 0.78 us: local(): by_x = sums[7:17].reshape(2, 5, IL)]
    pallas_call x0 -> x1, Pallas kernels: none -> 4.37 us  [finish(): pl.pallas_call(finish_kernel, out_shape=[jax.ShapeDtypeStruct(s, t) for s...]
where the time goes in v2:
time: 189 us; the launch traced here: 188 us
  Pallas kernels  188 us (99%)
    pallas_call x1, Pallas kernels, chain(): pl.pallas_call(chain_kernel, out_shape=[jax.ShapeDtypeStruct(s, t) for s,...  183 us
    pallas_call x1, Pallas kernels, finish(): pl.pallas_call(finish_kernel, out_shape=[jax.ShapeDtypeStruct(s, t) for s...  4.37 us

profile of v2, /device:TPU:1, one launch (start us, length us, event | category | flops | bytes accessed | tf_op | source)
XLA Modules:
  0.0 188.4 jit_solution(904248323711551096)
XLA Ops:
  0.7 183.2 %chain.1 = (bf16[128,2048]{1,0:T(8,128)(2,1)}, bf16[128,2048]{1,0:T(8,128)(2,1)}, f32[2,64,2,1024]{3,2,1,0:T(2,128)}, f32[2,64,1024]{2,1,0:T(8,128)}, f32[2,64,2...) custom-call(bf16[128,2048]{1,0:T(8,128)(2,1)} %refs_0_.1, bf16[128,2048]{1,0:T(8,128)(2,1)} %refs_1_.1, ...), custom_call_target="tpu_custom_call" | custom-call | tf_op jit(solution)/shard_map/chain/pallas_call | solution.py:1111
  183.9 4.4 %finish.1 = (bf16[128,2048]{1,0:T(8,128)(2,1)}, bf16[128,2048]{1,0:T(8,128)(2,1)}, f32[2,64]{1,0:T(2,128)}, f32[2,64,2,1024]{3,2,1,0:T(2,128)}, f32[2,64,256]{2,...) custom-call(bf16[128,2048]{1,0:T(8,128)(2,1)} %get-tuple-element.37., ...), custom_call_target="tpu_custom_call" | custom-call | tf_op jit(solution)/shard_map/finish/pallas_call | solution.py:1170
